TPU v7x, 256 devices: a whole 4x4x8 slice. The times are simulated.
256 devices in a mesh: section: 2 (over core), dp: 32 (over z, x), mp: 4 (over y).
Axes of the slice: x: 4, y: 4, z: 8, core: 2. Of those that a mesh axis runs over, the one named last changes fastest.
Arguments:
- prompt_state: bfloat16 [1024, 2048], P(('section', 'dp')), may hold values from -6 to 6
- beam_parent: int32 [1024, 4, 16], P(('section', 'dp')), may hold values from 0 to 15
- beam_code: int32 [1024, 4, 16], P(('section', 'dp')), may hold values from 0 to 255
- norm_gain: float32 [2048], replicated, may hold values from 0.1 to 1.9
- up_weight: bfloat16 [2048, 4096], P(None, 'mp'), may hold values from -0.125 to 0.125
- down_weight: bfloat16 [4096, 2048], P('mp'), may hold values from -0.09375 to 0.09375
- code_table: bfloat16 [256, 2048], replicated, may hold values from -6 to 6
- item_features: bfloat16 [32768, 1024], P('dp'), may hold values from -6 to 6
- lookup_owner: int32 [1024, 384, 1], P(('section', 'dp', 'mp')), may hold values from 0 to 31; in each aligned block of 1536 rows (0 to 1535, 1536 to 3071, ..., all dimensions but the last counted through in order) at most 96 rows name the same one
- lookup_row: int32 [1024, 384], P(('section', 'dp', 'mp')), may hold values from 0 to 1023
- cand_count: int32 [1024], P(('section', 'dp', 'mp')), may hold values from 16 to 128
- item_proj: bfloat16 [1024, 384], replicated, may hold values from -0.1875 to 0.1875
- user_proj: bfloat16 [2048, 256], replicated, may hold values from -0.125 to 0.125
- rank_bias: float32 [256], replicated, may hold values from -3 to 3
- out_weight: float32 [256], replicated, may hold values from -0.375 to 0.375
Outputs:
- logits: float32 [1024, 128], P(('section', 'dp', 'mp'))
- user_state: bfloat16 [1024, 2048], P(('section', 'dp'))
Inputs may be any that keep to these rules, and one draw needn't show every extreme that they name: `lookup_owner`: among the lookups of one device (1536 aligned rows) no owner is named more than 96 times, a bound that some block reaches.
All inputs are finite; a program needn't handle non-finite values.
Results may differ from a plain program's by a relative error of at most 0.035.
Values may be sent and summed in bfloat16 or wider, within the bound.
No kernel may reach another device: no remote copies, remote signals or barrier semaphores. Data moves between devices by JAX's collectives and lax.ppermute only.
A program may use at most 128 MiB of HBM per device.

v0:
```python
import functools
import math

import jax
import jax.numpy as jnp
from jax import lax
from jax.experimental import pallas as pl
from jax.experimental.pallas import tpu as pltpu
from jax.sharding import PartitionSpec as P

ATT = 128
CMAX = 128
HIST = 256
UP_CUTS = 4
DOWN_CUTS = 4
BF = jnp.bfloat16
F32 = jnp.float32
NT = (((1,), (1,)), ((), ()))

VMEM = pl.BlockSpec(memory_space=pltpu.VMEM)
SMEM = pl.BlockSpec(memory_space=pltpu.SMEM)
HBM = pl.BlockSpec(memory_space=pltpu.HBM)


def dot(a, b):
    return jnp.dot(a, b, preferred_element_type=F32)


def call(kernel, name, out_shape, in_specs, out_specs, scratch=(), limit=16, flops=0, moved=0):
    return pl.pallas_call(
        kernel,
        name=name,
        out_shape=out_shape,
        in_specs=in_specs,
        out_specs=out_specs,
        scratch_shapes=list(scratch),
        compiler_params=pltpu.CompilerParams(vmem_limit_bytes=limit * 2**20),
        cost_estimate=pl.CostEstimate(flops=flops, bytes_accessed=moved, transcendentals=0),
    )


def shift(value, axis, by):
    size = lax.axis_size(axis)
    return lax.ppermute(value, axis, [(i, (i + by) % size) for i in range(size)])


def swapped(value, axis, bit):
    mask = 2**bit
    pairs = [(source, source ^ mask) for source in range(lax.axis_size(axis))]
    return lax.ppermute(value, axis, pairs)


def after(value, earlier):
    return lax.optimization_barrier((value, earlier))[0]


def normalize(values, gain_row):
    squares = jnp.mean(values * values, axis=-1, keepdims=True)
    return values * lax.rsqrt(squares + 1e-06) * gain_row


def raise_rows(normed, up, act_s):
    wide = up.shape[1] // UP_CUTS
    for c in range(UP_CUTS):
        cut = slice(c * wide, (c + 1) * wide)
        act_s[:, cut] = jax.nn.gelu(dot(normed, up[:, cut])).astype(BF)


def start_kernel(
    owners, local_rows, prompt, gain, up, down,
    outgoing, target, part, prompt_v, gain_v, up_v, down_v, owners_s, local_s, act_s, sems,
):
    pairs = (
        (owners, owners_s), (local_rows, local_s), (prompt, prompt_v), (gain, gain_v),
        (up, up_v), (down, down_v),
    )
    copies = [pltpu.make_async_copy(a, b, sems.at[k]) for k, (a, b) in enumerate(pairs)]
    for copy in copies:
        copy.start()
    copies[0].wait()
    copies[1].wait()
    name_places(owners_s, local_s, outgoing, target)
    copies[2].wait()
    copies[3].wait()
    normed = normalize(prompt_v[...].astype(F32), gain_v[...]).astype(BF)
    copies[4].wait()
    raise_rows(normed, up_v, act_s)
    copies[5].wait()
    part[...] = dot(act_s[...], down_v[...]).astype(BF)


def load_kernel(up, down, up_v, down_v, sems):
    copies = [
        pltpu.make_async_copy(up, up_v, sems.at[0]),
        pltpu.make_async_copy(down, down_v, sems.at[1]),
    ]
    for copy in copies:
        copy.start()
    for copy in copies:
        copy.wait()


def lower(act_s, down, outs):
    tall = down.shape[1] // DOWN_CUTS
    own = outs[0].shape[0]
    for c in range(DOWN_CUTS):
        cut = slice(c * tall, (c + 1) * tall)
        part = dot(act_s[...], down[:, cut]).astype(BF)
        for k, out in enumerate(outs):
            out[:, cut] = part[k * own : (k + 1) * own, :]


def second_kernel(
    prompt, t0, t1, t2, t3, code_rows, gain, up, down,
    o0, o1, o2, o3, state, act_s, middle_s, normed_s,
):
    requests = prompt.shape[0]
    beams = code_rows.shape[0] // requests
    own = o0.shape[0]
    total = (
        t0[...].astype(F32) + t1[...].astype(F32) + t2[...].astype(F32) + t3[...].astype(F32)
    )
    middle = (prompt[...].astype(F32) + total).astype(BF).astype(F32)
    middle_s[0:requests, :] = middle
    middle_s[requests : 2 * requests, :] = middle
    base = lax.axis_index("mp") * (own // beams)
    for r in range(requests):
        row = middle_s[pl.ds(base + r, 1), :]
        now = (row + code_rows[r * beams : (r + 1) * beams, :].astype(F32)).astype(BF)
        if (r + 1) * beams <= own:
            state[r * beams : (r + 1) * beams, :] = now
        normed_s[r * beams : (r + 1) * beams, :] = normalize(now.astype(F32), gain[...]).astype(BF)
    raise_rows(normed_s[...], up, act_s)
    lower(act_s, down, (o0, o1, o2, o3))


def gathered(blocks, normed_s):
    own = blocks[0].shape[0]
    for k, ref in enumerate(blocks):
        normed_s[k * own : (k + 1) * own, :] = ref[...]
    return normed_s[...]


def third_kernel(n0, n1, n2, n3, up, down, o0, o1, o2, o3, act_s, normed_s):
    raise_rows(gathered((n0, n1, n2, n3), normed_s), up, act_s)
    lower(act_s, down, (o0, o1, o2, o3))


def last_kernel(n0, n1, n2, n3, pool, base, up, down, out, act_s, normed_s):
    raise_rows(gathered((n0, n1, n2, n3), normed_s), up, act_s)
    mixed = dot(pool[...], act_s[...]).astype(BF)
    out[...] = (dot(mixed, down[...]) + base[...]).astype(BF)


def advance(t0, t1, t2, t3, state, chosen, code_rows):
    total = (
        t0[...].astype(F32) + t1[...].astype(F32) + t2[...].astype(F32) + t3[...].astype(F32)
    )
    middle = (state[...].astype(F32) + total).astype(BF)
    return (dot(chosen[...], middle) + code_rows[...].astype(F32)).astype(BF)


def owner_kernel(t0, t1, t2, t3, state, chosen, code_rows, gain, out_state, out_normed):
    now = advance(t0, t1, t2, t3, state, chosen, code_rows)
    out_state[...] = now
    out_normed[...] = normalize(now.astype(F32), gain[...]).astype(BF)


def owner_last_kernel(
    t0, t1, t2, t3, state, chosen, code_rows, gain, pool, mean_code, out_base, out_normed
):
    now = advance(t0, t1, t2, t3, state, chosen, code_rows)
    out_normed[...] = normalize(now.astype(F32), gain[...]).astype(BF)
    rows = state.shape[0]
    out_base[...] = dot(pool[:, :rows], now) + mean_code[...]


def prepare_kernel(
    code, parent, table,
    rows0, rows1, rows2, mean_code, pool, chosen1, chosen2, code_s, parent_s, table_s, sems,
):
    pairs = ((code, code_s), (parent, parent_s), (table, table_s))
    copies = [pltpu.make_async_copy(a, b, sems.at[k]) for k, (a, b) in enumerate(pairs)]
    for copy in copies:
        copy.start()
    codes = table.shape[0]
    requests, _, beams = code.shape
    spots = requests * beams
    own = rows1.shape[0]
    base = lax.axis_index("mp") * (own // beams)
    row = lax.broadcasted_iota(jnp.int32, (spots, beams), 0)
    lane = lax.broadcasted_iota(jnp.int32, (spots, beams), 1)
    spread = (lane == (row // beams + base) % requests).astype(BF)
    kept = lane == row % beams

    def column(values):
        wide = dot(spread, values.astype(F32).astype(BF))
        return jnp.sum(jnp.where(kept, wide, 0.0), axis=1, keepdims=True).astype(jnp.int32)

    def picked(ids):
        names = lax.broadcasted_iota(jnp.int32, (ids.shape[0], codes), 1)
        return dot((ids == names).astype(BF), table_s[...]).astype(BF)

    copies[0].wait()
    columns = [column(code_s[:, k, :]) for k in range(3)]
    copies[1].wait()
    block = lax.broadcasted_iota(jnp.int32, (own, 1), 0) // beams * beams
    places = lax.broadcasted_iota(jnp.int32, (own, own), 1)
    for k, out in ((1, chosen1), (2, chosen2)):
        out[...] = (column(parent_s[:, k, :])[:own] + block == places).astype(BF)
    code3 = code_s[:, 3, :]
    parent3 = parent_s[:, 3, :]
    tally = jnp.zeros((requests, codes), F32)
    names = lax.broadcasted_iota(jnp.int32, (requests, codes), 1)
    kids = jnp.zeros((requests, spots), F32)
    lanes = lax.broadcasted_iota(jnp.int32, (requests, spots), 1)
    for b in range(beams):
        tally = tally + (code3[:, b : b + 1] == names).astype(F32)
        kids = kids + (parent3[:, b : b + 1] == lanes % beams).astype(F32)
    held = (base + lanes // beams) % requests
    mine = held == lax.broadcasted_iota(jnp.int32, (requests, spots), 0)
    pool[...] = jnp.where(mine, kids / beams, 0.0).astype(BF)
    number = lax.broadcasted_iota(jnp.int32, (requests, codes), 0)
    ours = (number >= base) & (number < base + own // beams)
    copies[2].wait()
    rows0[...] = picked(columns[0])
    rows1[...] = picked(columns[1][:own])
    rows2[...] = picked(columns[2][:own])
    mean_code[...] = dot(jnp.where(ours, tally / beams, 0.0).astype(BF), table_s[...])


def pool_kernel(t0, t1, t2, t3, out):
    out[...] = (
        t0[...].astype(F32) + t1[...].astype(F32) + t2[...].astype(F32) + t3[...].astype(F32)
    ).astype(BF)


def name_places(owners, local_rows, outgoing, target):
    requests, slots = local_rows.shape
    count, capacity = outgoing.shape
    before = (
        lax.broadcasted_iota(jnp.int32, (slots, slots), 0)
        < lax.broadcasted_iota(jnp.int32, (slots, slots), 1)
    ).astype(BF)
    names = lax.broadcasted_iota(jnp.int32, (count, slots), 0)
    places = lax.broadcasted_iota(jnp.int32, (128, slots), 0)
    carry = jnp.zeros((count, 1), F32)
    low = jnp.zeros((count, 128), F32)
    high = jnp.zeros((count, 128), F32)
    lines = []
    for q in range(requests):
        owner = owners[q]
        row = local_rows[q : q + 1, :]
        named = (owner == names).astype(F32)
        ahead = dot(named.astype(BF), before) + carry
        carry = carry + jnp.sum(named, axis=1, keepdims=True)
        position = jnp.sum(named * ahead, axis=0, keepdims=True).astype(jnp.int32)
        lines.append(owner * capacity + position)
        spot = (places == position).astype(BF)
        low = low + lax.dot_general(
            (named * (row & 31).astype(F32)).astype(BF), spot, NT, preferred_element_type=F32
        )
        high = high + lax.dot_general(
            (named * (row >> 5).astype(F32)).astype(BF), spot, NT, preferred_element_type=F32
        )
    outgoing[...] = (high * 32.0 + low).astype(jnp.int32)[:, :capacity]
    spare = jnp.zeros((target.shape[0] - requests, slots), jnp.int32)
    target[...] = jnp.concatenate(lines + [spare], axis=0)


def table_kernel(features, proj, table):
    table[...] = dot(features[...], proj[...]).astype(BF)


def serve_kernel(wanted, table, out, *, group):
    rows = table.shape[0]
    count, capacity, _ = out.shape
    asked = jnp.transpose(wanted[...])
    ids = lax.broadcasted_iota(jnp.int32, (capacity * group, rows), 1)
    for g in range(0, count, group):
        column = jnp.concatenate([asked[:, g + k : g + k + 1] for k in range(group)], axis=0)
        found = dot((column == ids).astype(BF), table[...]).astype(BF)
        for k in range(group):
            out[g + k] = found[k * capacity : (k + 1) * capacity, :]


def rank_kernel(target, returned, bias, user_proj, out, user_proj_v, sem):
    copy = pltpu.make_async_copy(user_proj, user_proj_v, sem)
    copy.start()
    requests = out.shape[0]
    count, capacity, width = returned.shape
    table = returned[...].reshape(count * capacity, width)
    targets = jnp.transpose(target[...])
    slots = targets.shape[0]
    ids = lax.broadcasted_iota(jnp.int32, (slots, count * capacity), 1)
    for q in range(requests):
        rows = dot((targets[:, q : q + 1] == ids).astype(BF), table).astype(BF)
        queries = rows[:CMAX, :ATT]
        keys = rows[CMAX:, :ATT]
        scores = lax.dot_general(queries, keys, NT, preferred_element_type=F32) / math.sqrt(ATT)
        weights = jax.nn.sigmoid(scores).astype(BF)
        interest = dot(weights, rows[CMAX:, ATT:]) / math.sqrt(HIST)
        out[q] = interest + rows[:CMAX, ATT:].astype(F32) + bias[...]
    copy.wait()


def logit_kernel(counts, users, user_proj, units, weight, out, term_s):
    term_s[...] = dot(users[...], user_proj[...])
    requests = units.shape[0]
    base = lax.axis_index("mp") * requests
    lanes = lax.broadcasted_iota(jnp.int32, (1, CMAX), 1)
    for q in range(requests):
        hidden = jnp.maximum(units[q] + term_s[pl.ds(base + q, 1), :], 0.0)
        line = lax.dot_general(
            weight[...], hidden, NT, preferred_element_type=F32, precision=lax.Precision.HIGHEST
        )
        out[q : q + 1, :] = jnp.where(lanes < counts[q], line, 0.0)


def body(
    prompt_state,
    beam_parent,
    beam_code,
    norm_gain,
    up_weight,
    down_weight,
    code_table,
    item_features,
    lookup_owner,
    lookup_row,
    cand_count,
    item_proj,
    user_proj,
    rank_bias,
    out_weight,
):
    requests, width = prompt_state.shape
    beams = beam_parent.shape[2]
    hidden = up_weight.shape[1]
    rows = requests * beams
    rank_rows, slots = lookup_row.shape
    own = rank_rows * beams
    owner_count = lax.axis_size("dp")
    capacity = max(2, 2 * rank_rows * slots // owner_count)
    columns = item_proj.shape[1]
    gain = norm_gain.reshape(1, width)
    shape = jax.ShapeDtypeStruct
    DMA = pltpu.SemaphoreType.DMA

    outgoing, target, part, prompt, gain, up, down = call(
        start_kernel, "start",
        (
            shape((owner_count, capacity), jnp.int32), shape((8, slots), jnp.int32),
            shape((requests, width), BF), shape((requests, width), BF), shape((1, width), F32),
            shape((width, hidden), BF), shape((hidden, width), BF),
        ),
        [HBM] * 6, (VMEM,) * 7,
        (
            pltpu.VMEM((rank_rows, 1, slots), jnp.int32), pltpu.VMEM((rank_rows, slots), jnp.int32),
            pltpu.VMEM((requests, hidden), BF), DMA((6,)),
        ),
        limit=40, flops=100 * rows * width * hidden, moved=1_000_000,
    )(
        jnp.transpose(lookup_owner, (0, 2, 1)), lookup_row, prompt_state, gain,
        up_weight, down_weight,
    )
    parts = [shift(part, "mp", k) for k in (1, 2, 3)]
    began = part
    rows0, rows1, rows2, mean_code, pool, chosen1, chosen2 = call(
        prepare_kernel, "prepare",
        (
            shape((rows, width), BF), shape((own, width), BF), shape((own, width), BF),
            shape((requests, width), F32), shape((requests, rows), BF),
            shape((own, own), BF), shape((own, own), BF),
        ),
        [HBM] * 3, (VMEM,) * 7,
        (
            pltpu.VMEM(beam_code.shape, jnp.int32), pltpu.VMEM(beam_parent.shape, jnp.int32),
            pltpu.VMEM(code_table.shape, BF), DMA((3,)),
        ),
        limit=16, flops=2 * 400 * 256 * width, moved=3_000_000,
    )(beam_code, after(beam_parent, part), code_table)
    ffn = dict(limit=16, flops=4 * rows * width * hidden, moved=50 * width * hidden)

    quarter = (shape((own, width), BF),) * 4
    *outs, state = call(
        second_kernel, "ffn1", quarter + (shape((own, width), BF),),
        [VMEM] * 9, (VMEM,) * 5,
        (pltpu.VMEM((rows, hidden), BF),
         pltpu.VMEM((2 * requests, width), F32), pltpu.VMEM((rows, width), BF)),
        **ffn,
    )(prompt, part, *parts, rows0, gain, up, down)
    outgoing = after(outgoing, outs[0])
    wanted = lax.all_to_all(outgoing, "dp", split_axis=0, concat_axis=0, tiled=True)
    sums = [outs[0]] + [shift(outs[k], "mp", k) for k in (1, 2, 3)]
    state, normed = call(
        owner_kernel, "owner1", (shape((own, width), BF),) * 2, [VMEM] * 8, (VMEM,) * 2,
        limit=16, flops=2 * own * own * width, moved=2_000_000,
    )(*sums, state, chosen1, rows1, gain)

    up, down = call(
        load_kernel, "load", (shape((width, hidden), BF), shape((hidden, width), BF)),
        [HBM] * 2, (VMEM,) * 2, (DMA((2,)),), limit=40, flops=20 * rows * width * hidden, moved=1_000_000,
    )(after(up_weight, normed), after(down_weight, normed))
    wanted = after(wanted, normed)
    others = [normed] + [shift(normed, "mp", -k) for k in (1, 2, 3)]
    outs = call(
        third_kernel, "ffn2", quarter, [VMEM] * 6, (VMEM,) * 4,
        (pltpu.VMEM((rows, hidden), BF), pltpu.VMEM((rows, width), BF)),
        **ffn,
    )(*others, up, down)
    sums = [outs[0]] + [shift(outs[k], "mp", k) for k in (1, 2, 3)]
    base, normed = call(
        owner_last_kernel, "owner2", (shape((requests, width), F32), shape((own, width), BF)),
        [VMEM] * 10, (VMEM,) * 2,
        limit=16, flops=2 * own * own * width, moved=2_000_000,
    )(*sums, state, chosen2, rows2, gain, pool, mean_code)

    others = [normed] + [shift(normed, "mp", -k) for k in (1, 2, 3)]
    part = call(
        last_kernel, "ffn3", shape((requests, width), BF), [VMEM] * 8, VMEM,
        (pltpu.VMEM((rows, hidden), BF), pltpu.VMEM((rows, width), BF)),
        **ffn,
    )(*others, pool, base, up, down)
    parts = [shift(part, "mp", k) for k in (1, 2, 3)]
    table = call(
        table_kernel, "table", shape((item_features.shape[0], columns), BF), [VMEM] * 2, VMEM,
        limit=16, flops=2 * item_features.size * columns, moved=4_000_000,
    )(item_features, after(item_proj, began))
    served = call(
        functools.partial(serve_kernel, group=4), "serve",
        shape((owner_count, capacity, columns), BF), [VMEM] * 2, VMEM, limit=16,
        flops=2 * owner_count * capacity * item_features.shape[0] * columns, moved=4_000_000,
    )(wanted, table)
    returned = lax.all_to_all(served, "dp", split_axis=0, concat_axis=0, tiled=True)
    returned = after(returned, part)
    units, user_proj = call(
        rank_kernel, "rank",
        (shape((rank_rows, CMAX, columns - ATT), F32), shape(user_proj.shape, BF)),
        [VMEM] * 3 + [HBM], (VMEM,) * 2, (DMA,), limit=16,
        flops=2 * rank_rows * slots * owner_count * capacity * columns, moved=4_000_000,
    )(target, returned, rank_bias.reshape(1, -1), user_proj)
    part_late = after(part, units)
    pooled = call(
        pool_kernel, "pool", shape((requests, width), BF), [VMEM] * 4, VMEM,
        limit=16, flops=100_000, moved=400_000,
    )(part_late, *parts)
    partner = swapped(pooled, "section", 0)

    logits = call(
        logit_kernel, "logit", shape((rank_rows, CMAX), F32), [SMEM] + [VMEM] * 4, VMEM,
        (pltpu.VMEM((requests, user_proj.shape[1]), F32),),
        limit=16, flops=20_000_000, moved=1_600_000,
    )(cand_count, partner, user_proj, units, out_weight.reshape(1, -1))
    return (logits, pooled)


def solution(mesh):
    in_specs = (
        P(("section", "dp"), None),
        P(("section", "dp"), None, None),
        P(("section", "dp"), None, None),
        P(),
        P(None, "mp"),
        P("mp", None),
        P(),
        P("dp", None),
        P(("section", "dp", "mp"), None, None),
        P(("section", "dp", "mp"), None),
        P(("section", "dp", "mp")),
        P(),
        P(),
        P(),
        P(),
    )
    out_specs = (P(("section", "dp", "mp"), None), P(("section", "dp"), None))
    return jax.shard_map(body, mesh=mesh, in_specs=in_specs, out_specs=out_specs, check_vma=False)
```

profile of v0, /device:TPU:1, one launch (start us, length us, event | category | flops | bytes accessed | tf_op | source)
XLA Modules:
  0.0 129.4 jit_solution(10018083866317659608)
XLA Ops:
  0.6 2.2 %copy-done.16 = bf16[2048,1024]{1,0:T(8,128)(2,1)S(1)} copy-done((bf16[2048,1024]{1,0:T(8,128)(2,1)S(1)}, bf16[2048,1024]{1,0:T(8,128)(2,1)}, u32[]{:S(2)}) %copy-start.16) | copy-done | bytes 4194328
  2.8 0.8 copy-done.20
  3.7 0.7 copy-done.23
  4.4 0.7 copy-done.24
  5.1 0.7 copy-done.25
  5.8 3.3 %start.1 = (s32[32,96]{1,0:T(8,128)S(1)}, s32[8,384]{1,0:T(8,128)S(1)}, bf16[16,2048]{1,0:T(8,128)(2,1)S(1)}, bf16[16,2048]{1,0:T(8,128)(2,1)S(1)}, f32[1,2048]{...) custom-call(s32[4,1,384]{2,1,0:T(1,128)S(1)} %bitcast.11, s32[4,384]{1,0:T(4,128)S(1)} %copy-done.25, ...), custom_call_target="tpu_custom_call" | custom-call | flops 53687091200 | bytes 1000000 | tf_op jit(solution)/shard_map/start/pallas_call | solution.py:350
  10.2 2.1 %collective-permute-start = (bf16[16,2048]{1,0:T(8,128)(2,1)S(1)}, bf16[16,2048]{1,0:T(8,128)(2,1)S(1)}, u32[]{:S(2)}, u32[]{:S(2)}) collective-permute-start(bf16[16,2048]{1,0:T(8,128)(2,1)S(1)} %get-tuple-element.42.t0), channel_id=1, source_target_pairs={{0,1},{1,2},{2,3},{3,0},{4,5},{5,6},{6,7},{7,4},{8,9},{9,10},{10,1... | collective-permute-start | bytes 196616 | tf_op jit(solution)/shard_map/ppermute | solution.py:44
  12.4 2.6 %collective-permute-start.1 = (bf16[16,2048]{1,0:T(8,128)(2,1)S(1)}, bf16[16,2048]{1,0:T(8,128)(2,1)S(1)}, u32[]{:S(2)}, u32[]{:S(2)}) collective-permute-start(bf16[16,2048]{1,0:T(8,128)(2,1)S(1)} %get-tuple-element.42.t0), channel_id=1, source_target_pairs={{0,2},{1,3},{2,0},{3,1},{4,6},{5,7},{6,4},{7,5},{8,10},{9,11},{10,... | collective-permute-start | bytes 196616 | tf_op jit(solution)/shard_map/ppermute | solution.py:44
  15.0 1.1 collective-permute-start.2
  16.1 2.1 %prepare.1 = (bf16[256,2048]{1,0:T(8,128)(2,1)S(1)}, bf16[64,2048]{1,0:T(8,128)(2,1)S(1)}, bf16[64,2048]{1,0:T(8,128)(2,1)S(1)}, f32[16,2048]{1,0:T(8,128)S(1)},...) custom-call(s32[16,4,16]{2,1,0:T(4,128)S(1)} %copy-done.21, ...), custom_call_target="tpu_custom_call" | custom-call | flops 419430400 | bytes 3000000 | tf_op jit(solution)/shard_map/prepare/pallas_call | solution.py:369
  18.4 3.7 %ffn1.1 = (bf16[64,2048]{1,0:T(8,128)(2,1)S(1)}, bf16[64,2048]{1,0:T(8,128)(2,1)}, bf16[64,2048]{1,0:T(8,128)(2,1)}, bf16[64,2048]{1,0:T(8,128)(2,1)}, bf16[64,2048]{1,0:T(8,128)(2,1)S(1)}) custom-call(bf16[16,2048]{1,0:T(8,128)(2,1)S(1)} %get-tuple-element.41.prompt, bf16[16,2048]{1,0:T(8,128)(2,1)S(1)} %get-tuple-element.42.t0, ...), custom_call_target="tpu_custom_call" | custom-call | flops 2147483648 | bytes 104857600 | tf_op jit(solution)/shard_map/ffn1/pallas_call | solution.py:386
  22.1 0.7 copy-done.5
  23.2 2.9 %collective-permute-start.4 = (bf16[64,2048]{1,0:T(8,128)(2,1)}, bf16[64,2048]{1,0:T(8,128)(2,1)}, u32[]{:S(2)}, u32[]{:S(2)}) collective-permute-start(bf16[64,2048]{1,0:T(8,128)(2,1)} %get-tuple-element.50), channel_id=1, source_target_pairs={{0,2},{1,3},{2,0},{3,1},{4,6},{5,7},{6,4},{7,5},{8,10},{9,11},{10,... | collective-permute-start | bytes 786440 | tf_op jit(solution)/shard_map/ppermute | solution.py:44
  26.2 11.3 %all-to-all-start = ((s32[32,1,96]{2,1,0:T(1,128)}), s32[32,1,96]{2,1,0:T(1,128)}, u32[]{:S(2)}, u32[]{:S(2)}) async-start(s32[32,1,96]{2,1,0:T(1,128)} %bitcast.8), calls=%async_computation | async-start | bytes 32768 | tf_op jit(solution)/shard_map/all_to_all | solution.py:394
  37.5 1.2 table.3
  38.8 0.9 copy-done.3
  39.7 0.9 copy-done.6
  40.7 0.7 copy-done.12
  41.4 1.6 %owner1.1 = (bf16[64,2048]{1,0:T(8,128)(2,1)S(1)}, bf16[64,2048]{1,0:T(8,128)(2,1)S(1)}) custom-call(bf16[64,2048]{1,0:T(8,128)(2,1)S(1)} %get-tuple-element.48.t0, bf16[64,2048]{1,0:T(8,128)(2,1)} %collective-permute-done.3.t1, bf16[64,2048]{1,0:T(8,128)(2,1)} %collective-permute-done.4.t2, bf16[64,2048]{1,0:T(8,128)(2,1)} %collective-permute-done.5.t3, ...), custom_call_target="tpu_custom_call" | custom-call | flops 16777216 | bytes 2000000 | tf_op jit(solution)/shard_map/owner1/pallas_call | solution.py:396
  43.0 2.6 %all-to-all-done = s32[32,1,96]{2,1,0:T(1,128)} async-done(((s32[32,1,96]{2,1,0:T(1,128)}), s32[32,1,96]{2,1,0:T(1,128)}, u32[]{:S(2)}, u32[]{:S(2)}) %all-to-all-start) | async-done | bytes 12320 | tf_op jit(solution)/shard_map/all_to_all | solution.py:394
  45.6 1.1 copy-done.4
  46.7 4.3 %serve.1 = bf16[32,96,384]{2,1,0:T(8,128)(2,1)S(1)} custom-call(s32[32,96]{1,0:T(8,128)} %bitcast.4.wanted, bf16[1024,384]{1,0:T(8,128)(2,1)S(1)} %copy-done.4), custom_call_target="tpu_custom_call" | custom-call | flops 2415919104 | bytes 4000000 | tf_op jit(solution)/shard_map/serve/pallas_call | solution.py:430
  51.1 1.4 %copy-done = bf16[32,96,384]{2,1,0:T(8,128)(2,1)} copy-done((bf16[32,96,384]{2,1,0:T(8,128)(2,1)}, bf16[32,96,384]{2,1,0:T(8,128)(2,1)S(1)}, u32[]{:S(2)}) %copy-start) | copy-done | bytes 2359320
  52.5 6.4 %all-to-all-start.1 = ((bf16[32,96,384]{2,1,0:T(8,128)(2,1)}), bf16[32,96,384]{2,1,0:T(8,128)(2,1)S(1)}, u32[]{:S(2)}, u32[]{:S(2)}) async-start(bf16[32,96,384]{2,1,0:T(8,128)(2,1)} %copy-done), calls=%async_computation.1 | async-start | bytes 4718592 | tf_op jit(solution)/shard_map/all_to_all | solution.py:435
  58.8 3.3 %collective-permute-start.6 = (bf16[64,2048]{1,0:T(8,128)(2,1)S(1)}, bf16[64,2048]{1,0:T(8,128)(2,1)S(1)}, u32[]{:S(2)}, u32[]{:S(2)}) collective-permute-start(bf16[64,2048]{1,0:T(8,128)(2,1)S(1)} %get-tuple-element.55.n0), channel_id=1, source_target_pairs={{0,3},{1,0},{2,1},{3,2},{4,7},{5,4},{6,5},{7,6},{8,11},{9,8},{10,9... | collective-permute-start | bytes 786440 | tf_op jit(solution)/shard_map/ppermute | solution.py:44
  62.2 0.7 collective-permute-start.8
  62.8 2.2 %copy-done.17 = bf16[2048,1024]{1,0:T(8,128)(2,1)S(1)} copy-done((bf16[2048,1024]{1,0:T(8,128)(2,1)S(1)}, bf16[2048,1024]{1,0:T(8,128)(2,1)}, u32[]{:S(2)}) %copy-start.17) | copy-done | bytes 4194328
  65.0 2.5 %load.1 = (bf16[2048,1024]{1,0:T(8,128)(2,1)S(1)}, bf16[1024,2048]{1,0:T(8,128)(2,1)S(1)}) custom-call(bf16[2048,1024]{1,0:T(8,128)(2,1)S(1)} %copy-done.17, bf16[1024,2048]{1,0:T(8,128)(2,1)} %down.2), custom_call_target="tpu_custom_call" | custom-call | flops 10737418240 | bytes 1000000 | tf_op jit(solution)/shard_map/load/pallas_call | solution.py:401
  67.5 5.3 %collective-permute-done.6.n1 = bf16[64,2048]{1,0:T(8,128)(2,1)S(1)} collective-permute-done((bf16[64,2048]{1,0:T(8,128)(2,1)S(1)}, bf16[64,2048]{1,0:T(8,128)(2,1)S(1)}, u32[]{:S(2)}, u32[]{:S(2)}) %collective-permute-start.6) | collective-permute-done | bytes 262176 | tf_op jit(solution)/shard_map/ppermute | solution.py:44
  72.8 3.6 %collective-permute-done.8.n3 = bf16[64,2048]{1,0:T(8,128)(2,1)S(1)} collective-permute-done((bf16[64,2048]{1,0:T(8,128)(2,1)S(1)}, bf16[64,2048]{1,0:T(8,128)(2,1)S(1)}, u32[]{:S(2)}, u32[]{:S(2)}) %collective-permute-start.8) | collective-permute-done | bytes 262176 | tf_op jit(solution)/shard_map/ppermute | solution.py:44
  76.5 2.5 %ffn2.1 = (bf16[64,2048]{1,0:T(8,128)(2,1)S(1)}, bf16[64,2048]{1,0:T(8,128)(2,1)S(1)}, bf16[64,2048]{1,0:T(8,128)(2,1)S(1)}, bf16[64,2048]{1,0:T(8,128)(2,1)S(1)}) custom-call(bf16[64,2048]{1,0:T(8,128)(2,1)S(1)} %get-tuple-element.55.n0, bf16[64,2048]{1,0:T(8,128)(2,1)S(1)} %collective-permute-done.6.n1, bf16[64,2048]{1,0:T(8,128)(2,1)S(1)} %collective-permute-done.7.n2, ...), custom_call_target="tpu_custom_call" | custom-call | flops 2147483648 | bytes 104857600 | tf_op jit(solution)/shard_map/ffn2/pallas_call | solution.py:407
  79.1 1.1 collective-permute-start.10
  80.2 1.6 %collective-permute-start.11 = (bf16[64,2048]{1,0:T(8,128)(2,1)S(1)}, bf16[64,2048]{1,0:T(8,128)(2,1)S(1)}, u32[]{:S(2)}, u32[]{:S(2)}) collective-permute-start(bf16[64,2048]{1,0:T(8,128)(2,1)S(1)} %get-tuple-element.63), channel_id=1, source_target_pairs={{0,3},{1,0},{2,1},{3,2},{4,7},{5,4},{6,5},{7,6},{8,11},{9,8},{10,9... | collective-permute-start | bytes 786440 | tf_op jit(solution)/shard_map/ppermute | solution.py:44
  81.8 7.4 %collective-permute-done.9.t1 = bf16[64,2048]{1,0:T(8,128)(2,1)S(1)} collective-permute-done((bf16[64,2048]{1,0:T(8,128)(2,1)S(1)}, bf16[64,2048]{1,0:T(8,128)(2,1)S(1)}, u32[]{:S(2)}, u32[]{:S(2)}) %collective-permute-start.9) | collective-permute-done | bytes 262176 | tf_op jit(solution)/shard_map/ppermute | solution.py:44
  89.2 1.1 collective-permute-done.10.t2
  90.2 2.8 %collective-permute-done.11.t3 = bf16[64,2048]{1,0:T(8,128)(2,1)S(1)} collective-permute-done((bf16[64,2048]{1,0:T(8,128)(2,1)S(1)}, bf16[64,2048]{1,0:T(8,128)(2,1)S(1)}, u32[]{:S(2)}, u32[]{:S(2)}) %collective-permute-start.11) | collective-permute-done | bytes 262176 | tf_op jit(solution)/shard_map/ppermute | solution.py:44
  93.6 3.5 %collective-permute-start.12 = (bf16[64,2048]{1,0:T(8,128)(2,1)S(1)}, bf16[64,2048]{1,0:T(8,128)(2,1)S(1)}, u32[]{:S(2)}, u32[]{:S(2)}) collective-permute-start(bf16[64,2048]{1,0:T(8,128)(2,1)S(1)} %get-tuple-element.69.n0), channel_id=1, source_target_pairs={{0,3},{1,0},{2,1},{3,2},{4,7},{5,4},{6,5},{7,6},{8,11},{9,8},{10,9... | collective-permute-start | bytes 786440 | tf_op jit(solution)/shard_map/ppermute | solution.py:44
  97.1 0.9 collective-permute-start.14
  97.9 9.5 %collective-permute-done.12.n1 = bf16[64,2048]{1,0:T(8,128)(2,1)S(1)} collective-permute-done((bf16[64,2048]{1,0:T(8,128)(2,1)S(1)}, bf16[64,2048]{1,0:T(8,128)(2,1)S(1)}, u32[]{:S(2)}, u32[]{:S(2)}) %collective-permute-start.12) | collective-permute-done | bytes 262176 | tf_op jit(solution)/shard_map/ppermute | solution.py:44
  107.4 4.4 %collective-permute-done.14.n3 = bf16[64,2048]{1,0:T(8,128)(2,1)S(1)} collective-permute-done((bf16[64,2048]{1,0:T(8,128)(2,1)S(1)}, bf16[64,2048]{1,0:T(8,128)(2,1)S(1)}, u32[]{:S(2)}, u32[]{:S(2)}) %collective-permute-start.14) | collective-permute-done | bytes 262176 | tf_op jit(solution)/shard_map/ppermute | solution.py:44
  111.8 2.1 %ffn3.1.t0 = bf16[16,2048]{1,0:T(8,128)(2,1)S(1)} custom-call(bf16[64,2048]{1,0:T(8,128)(2,1)S(1)} %get-tuple-element.69.n0, bf16[64,2048]{1,0:T(8,128)(2,1)S(1)} %collective-permute-done.12.n1, bf16[64,2048]{1,0:T(8,128)(2,1)S(1)} %collective-permute-done.13.n2, bf16[64,2048]{1,0:T(8,128)(2,1)S(1)} %collective-permute-done.14.n3, ...), custom_call_target="tpu_custom_call" | custom-call | flops 2147483648 | bytes 104857600 | tf_op jit(solution)/shard_map/ffn3/pallas_call | solution.py:420
  114.0 0.7 collective-permute-start.16
  114.6 2.0 %collective-permute-start.17 = (bf16[16,2048]{1,0:T(8,128)(2,1)S(1)}, bf16[16,2048]{1,0:T(8,128)(2,1)S(1)}, u32[]{:S(2)}, u32[]{:S(2)}) collective-permute-start(bf16[16,2048]{1,0:T(8,128)(2,1)S(1)} %ffn3.1.t0), channel_id=1, source_target_pairs={{0,3},{1,0},{2,1},{3,2},{4,7},{5,4},{6,5},{7,6},{8,11},{9,8},{10,9... | collective-permute-start | bytes 196616 | tf_op jit(solution)/shard_map/ppermute | solution.py:44
  116.7 1.2 copy-done.19
  117.9 6.1 %rank.1 = (f32[4,128,256]{2,1,0:T(8,128)S(1)}, bf16[2048,256]{1,0:T(8,128)(2,1)S(1)}) custom-call(s32[8,384]{1,0:T(8,128)S(1)} %copy-done.28, bf16[32,96,384]{2,1,0:T(8,128)(2,1)S(1)} %all-to-all-done.1.returned, f32[1,256]{1,0:T(1,128)S(1)} %bitcast.12, bf16[2048,256]{1,0:T(8,128)(2,1)S(1)} %copy-done.19), custom_call_target="tpu_custom_call" | custom-call | flops 3623878656 | bytes 4000000 | tf_op jit(solution)/shard_map/rank/pallas_call | solution.py:437
  124.7 1.4 %collective-permute-start.18 = (bf16[16,2048]{1,0:T(8,128)(2,1)}, bf16[16,2048]{1,0:T(8,128)(2,1)S(1)}, u32[]{:S(2)}, u32[]{:S(2)}) collective-permute-start(bf16[16,2048]{1,0:T(8,128)(2,1)} %pool.1), channel_id=1, source_target_pairs={{0,128},{128,0},{1,129},{129,1},{2,130},{130,2},{3,131},{131,3},{4... | collective-permute-start | bytes 196616 | tf_op jit(solution)/shard_map/ppermute | solution.py:50
  126.1 1.1 collective-permute-done.18.users
  127.2 2.2 %logit.1 = f32[4,128]{1,0:T(4,128)} custom-call(s32[4]{0:T(128)S(1)} %copy-done.15, bf16[16,2048]{1,0:T(8,128)(2,1)S(1)} %collective-permute-done.18.users, bf16[2048,256]{1,0:T(8,128)(2,1)S(1)} %get-tuple-element.79.user_proj, f32[4,128,256]{2,1,0:T(8,128)S(1)} %get-tuple-element.77.units, f32[1,256]{1,0:T(1,128)S(1)} %bitcast.9), custom_call_target="tpu_custom_call" | custom-call | flops 20000000 | bytes 1600000 | tf_op jit(solution)/shard_map/logit/pallas_call | solution.py:450
  (65 shorter events, 3.2 us)
Async XLA Ops:
  0.6 2.2 %copy-start.16 = (bf16[2048,1024]{1,0:T(8,128)(2,1)S(1)}, bf16[2048,1024]{1,0:T(8,128)(2,1)}, u32[]{:S(2)}) copy-start(bf16[2048,1024]{1,0:T(8,128)(2,1)} %up.2) | copy-start | bytes 12582916
  2.8 0.8 copy-start.20
  3.7 0.7 copy-start.23
  4.4 0.7 copy-start.24
  5.1 0.7 copy-start.25
  5.7 10.3 %copy-start.18 = (bf16[256,2048]{1,0:T(8,128)(2,1)S(1)}, bf16[256,2048]{1,0:T(8,128)(2,1)}, u32[]{:S(2)}) copy-start(bf16[256,2048]{1,0:T(8,128)(2,1)} %table.2) | copy-start | bytes 3145732
  5.7 10.3 %copy-start.21 = (s32[16,4,16]{2,1,0:T(4,128)S(1)}, s32[16,4,16]{2,1,0:T(4,128)}, u32[]{:S(2)}) copy-start(s32[16,4,16]{2,1,0:T(4,128)} %code.1) | copy-start | bytes 12292
  5.7 10.3 %copy-start.22 = (s32[16,4,16]{2,1,0:T(4,128)S(1)}, s32[16,4,16]{2,1,0:T(4,128)}, u32[]{:S(2)}) copy-start(s32[16,4,16]{2,1,0:T(4,128)} %parent) | copy-start | bytes 12292
  10.2 8.0 %collective-permute-start = (bf16[16,2048]{1,0:T(8,128)(2,1)S(1)}, bf16[16,2048]{1,0:T(8,128)(2,1)S(1)}, u32[]{:S(2)}, u32[]{:S(2)}) collective-permute-start(bf16[16,2048]{1,0:T(8,128)(2,1)S(1)} %get-tuple-element.42.t0), channel_id=1, source_target_pairs={{0,1},{1,2},{2,3},{3,0},{4,5},{5,6},{6,7},{7,4},{8,9},{9,10},{10,1... | collective-permute-start | bytes 196616 | tf_op jit(solution)/shard_map/ppermute | solution.py:44
  12.4 5.9 %collective-permute-start.1 = (bf16[16,2048]{1,0:T(8,128)(2,1)S(1)}, bf16[16,2048]{1,0:T(8,128)(2,1)S(1)}, u32[]{:S(2)}, u32[]{:S(2)}) collective-permute-start(bf16[16,2048]{1,0:T(8,128)(2,1)S(1)} %get-tuple-element.42.t0), channel_id=1, source_target_pairs={{0,2},{1,3},{2,0},{3,1},{4,6},{5,7},{6,4},{7,5},{8,10},{9,11},{10,... | collective-permute-start | bytes 196616 | tf_op jit(solution)/shard_map/ppermute | solution.py:44
  15.0 3.4 %collective-permute-start.2 = (bf16[16,2048]{1,0:T(8,128)(2,1)S(1)}, bf16[16,2048]{1,0:T(8,128)(2,1)S(1)}, u32[]{:S(2)}, u32[]{:S(2)}) collective-permute-start(bf16[16,2048]{1,0:T(8,128)(2,1)S(1)} %get-tuple-element.42.t0), channel_id=1, source_target_pairs={{0,3},{1,0},{2,1},{3,2},{4,7},{5,4},{6,5},{7,6},{8,11},{9,8},{10,9... | collective-permute-start | bytes 196616 | tf_op jit(solution)/shard_map/ppermute | solution.py:44
  18.2 3.9 %copy-start.7 = (bf16[64,2048]{1,0:T(8,128)(2,1)}, bf16[64,2048]{1,0:T(8,128)(2,1)S(1)}, u32[]{:S(2)}) copy-start(bf16[64,2048]{1,0:T(8,128)(2,1)S(1)} %get-tuple-element.66.code_rows) | copy-start | bytes 786436
  18.2 3.9 %copy-start.9 = (bf16[64,64]{1,0:T(8,128)(2,1)}, bf16[64,64]{1,0:T(8,128)(2,1)S(1)}, u32[]{:S(2)}) copy-start(bf16[64,64]{1,0:T(8,128)(2,1)S(1)} %get-tuple-element.65.chosen) | copy-start | bytes 24580
  18.2 3.9 %copy-start.11 = (bf16[64,64]{1,0:T(8,128)(2,1)}, bf16[64,64]{1,0:T(8,128)(2,1)S(1)}, u32[]{:S(2)}) copy-start(bf16[64,64]{1,0:T(8,128)(2,1)S(1)} %get-tuple-element.53.chosen) | copy-start | bytes 24580
  18.4 19.1 %copy-start.1 = (bf16[1024,1024]{1,0:T(8,128)(2,1)S(1)}, bf16[1024,1024]{1,0:T(8,128)(2,1)}, u32[]{:S(2)}) copy-start(bf16[1024,1024]{1,0:T(8,128)(2,1)} %features.1) | copy-start | bytes 6291460
  18.4 19.1 %copy-start.2 = (bf16[1024,384]{1,0:T(8,128)(2,1)S(1)}, bf16[1024,384]{1,0:T(8,128)(2,1)}, u32[]{:S(2)}) copy-start(bf16[1024,384]{1,0:T(8,128)(2,1)} %proj) | copy-start | bytes 2359300
  22.1 0.7 copy-start.5
  22.9 16.9 %collective-permute-start.3 = (bf16[64,2048]{1,0:T(8,128)(2,1)}, bf16[64,2048]{1,0:T(8,128)(2,1)}, u32[]{:S(2)}, u32[]{:S(2)}) collective-permute-start(bf16[64,2048]{1,0:T(8,128)(2,1)} %get-tuple-element.49), channel_id=1, source_target_pairs={{0,1},{1,2},{2,3},{3,0},{4,5},{5,6},{6,7},{7,4},{8,9},{9,10},{10,1... | collective-permute-start | bytes 786440 | tf_op jit(solution)/shard_map/ppermute | solution.py:44
  23.2 16.5 %collective-permute-start.4 = (bf16[64,2048]{1,0:T(8,128)(2,1)}, bf16[64,2048]{1,0:T(8,128)(2,1)}, u32[]{:S(2)}, u32[]{:S(2)}) collective-permute-start(bf16[64,2048]{1,0:T(8,128)(2,1)} %get-tuple-element.50), channel_id=1, source_target_pairs={{0,2},{1,3},{2,0},{3,1},{4,6},{5,7},{6,4},{7,5},{8,10},{9,11},{10,... | collective-permute-start | bytes 786440 | tf_op jit(solution)/shard_map/ppermute | solution.py:44
  26.1 13.7 %collective-permute-start.5 = (bf16[64,2048]{1,0:T(8,128)(2,1)}, bf16[64,2048]{1,0:T(8,128)(2,1)}, u32[]{:S(2)}, u32[]{:S(2)}) collective-permute-start(bf16[64,2048]{1,0:T(8,128)(2,1)} %get-tuple-element.51), channel_id=1, source_target_pairs={{0,3},{1,0},{2,1},{3,2},{4,7},{5,4},{6,5},{7,6},{8,11},{9,8},{10,9... | collective-permute-start | bytes 786440 | tf_op jit(solution)/shard_map/ppermute | solution.py:44
  26.2 19.4 %all-to-all-start = ((s32[32,1,96]{2,1,0:T(1,128)}), s32[32,1,96]{2,1,0:T(1,128)}, u32[]{:S(2)}, u32[]{:S(2)}) async-start(s32[32,1,96]{2,1,0:T(1,128)} %bitcast.8), calls=%async_computation | async-start | bytes 32768 | tf_op jit(solution)/shard_map/all_to_all | solution.py:394
  38.8 0.9 copy-start.3
  39.7 1.0 copy-start.6
  40.7 0.7 copy-start.12
  45.6 1.1 copy-start.4
  51.1 1.4 %copy-start = (bf16[32,96,384]{2,1,0:T(8,128)(2,1)}, bf16[32,96,384]{2,1,0:T(8,128)(2,1)S(1)}, u32[]{:S(2)}) copy-start(bf16[32,96,384]{2,1,0:T(8,128)(2,1)S(1)} %serve.1) | copy-start | bytes 7077892
  52.5 64.2 %all-to-all-start.1 = ((bf16[32,96,384]{2,1,0:T(8,128)(2,1)}), bf16[32,96,384]{2,1,0:T(8,128)(2,1)S(1)}, u32[]{:S(2)}, u32[]{:S(2)}) async-start(bf16[32,96,384]{2,1,0:T(8,128)(2,1)} %copy-done), calls=%async_computation.1 | async-start | bytes 4718592 | tf_op jit(solution)/shard_map/all_to_all | solution.py:435
  58.8 14.0 %collective-permute-start.6 = (bf16[64,2048]{1,0:T(8,128)(2,1)S(1)}, bf16[64,2048]{1,0:T(8,128)(2,1)S(1)}, u32[]{:S(2)}, u32[]{:S(2)}) collective-permute-start(bf16[64,2048]{1,0:T(8,128)(2,1)S(1)} %get-tuple-element.55.n0), channel_id=1, source_target_pairs={{0,3},{1,0},{2,1},{3,2},{4,7},{5,4},{6,5},{7,6},{8,11},{9,8},{10,9... | collective-permute-start | bytes 786440 | tf_op jit(solution)/shard_map/ppermute | solution.py:44
  62.1 10.7 %collective-permute-start.7 = (bf16[64,2048]{1,0:T(8,128)(2,1)S(1)}, bf16[64,2048]{1,0:T(8,128)(2,1)S(1)}, u32[]{:S(2)}, u32[]{:S(2)}) collective-permute-start(bf16[64,2048]{1,0:T(8,128)(2,1)S(1)} %get-tuple-element.55.n0), channel_id=1, source_target_pairs={{0,2},{1,3},{2,0},{3,1},{4,6},{5,7},{6,4},{7,5},{8,10},{9,11},{10,... | collective-permute-start | bytes 786440 | tf_op jit(solution)/shard_map/ppermute | solution.py:44
  62.2 14.3 %collective-permute-start.8 = (bf16[64,2048]{1,0:T(8,128)(2,1)S(1)}, bf16[64,2048]{1,0:T(8,128)(2,1)S(1)}, u32[]{:S(2)}, u32[]{:S(2)}) collective-permute-start(bf16[64,2048]{1,0:T(8,128)(2,1)S(1)} %get-tuple-element.55.n0), channel_id=1, source_target_pairs={{0,1},{1,2},{2,3},{3,0},{4,5},{5,6},{6,7},{7,4},{8,9},{9,10},{10,1... | collective-permute-start | bytes 786440 | tf_op jit(solution)/shard_map/ppermute | solution.py:44
  62.8 2.2 %copy-start.17 = (bf16[2048,1024]{1,0:T(8,128)(2,1)S(1)}, bf16[2048,1024]{1,0:T(8,128)(2,1)}, u32[]{:S(2)}) copy-start(bf16[2048,1024]{1,0:T(8,128)(2,1)} %up.2) | copy-start | bytes 12582916
  76.5 16.6 %copy-start.8 = (bf16[64,2048]{1,0:T(8,128)(2,1)S(1)}, bf16[64,2048]{1,0:T(8,128)(2,1)}, u32[]{:S(2)}) copy-start(bf16[64,2048]{1,0:T(8,128)(2,1)} %copy-done.7) | copy-start | bytes 786436
  76.5 16.6 %copy-start.10 = (bf16[64,64]{1,0:T(8,128)(2,1)S(1)}, bf16[64,64]{1,0:T(8,128)(2,1)}, u32[]{:S(2)}) copy-start(bf16[64,64]{1,0:T(8,128)(2,1)} %copy-done.9) | copy-start | bytes 24580
  79.0 10.2 %collective-permute-start.9 = (bf16[64,2048]{1,0:T(8,128)(2,1)S(1)}, bf16[64,2048]{1,0:T(8,128)(2,1)S(1)}, u32[]{:S(2)}, u32[]{:S(2)}) collective-permute-start(bf16[64,2048]{1,0:T(8,128)(2,1)S(1)} %get-tuple-element.61), channel_id=1, source_target_pairs={{0,1},{1,2},{2,3},{3,0},{4,5},{5,6},{6,7},{7,4},{8,9},{9,10},{10,1... | collective-permute-start | bytes 786440 | tf_op jit(solution)/shard_map/ppermute | solution.py:44
  79.1 11.1 %collective-permute-start.10 = (bf16[64,2048]{1,0:T(8,128)(2,1)S(1)}, bf16[64,2048]{1,0:T(8,128)(2,1)S(1)}, u32[]{:S(2)}, u32[]{:S(2)}) collective-permute-start(bf16[64,2048]{1,0:T(8,128)(2,1)S(1)} %get-tuple-element.62), channel_id=1, source_target_pairs={{0,2},{1,3},{2,0},{3,1},{4,6},{5,7},{6,4},{7,5},{8,10},{9,11},{10,... | collective-permute-start | bytes 786440 | tf_op jit(solution)/shard_map/ppermute | solution.py:44
  80.2 12.9 %collective-permute-start.11 = (bf16[64,2048]{1,0:T(8,128)(2,1)S(1)}, bf16[64,2048]{1,0:T(8,128)(2,1)S(1)}, u32[]{:S(2)}, u32[]{:S(2)}) collective-permute-start(bf16[64,2048]{1,0:T(8,128)(2,1)S(1)} %get-tuple-element.63), channel_id=1, source_target_pairs={{0,3},{1,0},{2,1},{3,2},{4,7},{5,4},{6,5},{7,6},{8,11},{9,8},{10,9... | collective-permute-start | bytes 786440 | tf_op jit(solution)/shard_map/ppermute | solution.py:44
  93.6 13.9 %collective-permute-start.12 = (bf16[64,2048]{1,0:T(8,128)(2,1)S(1)}, bf16[64,2048]{1,0:T(8,128)(2,1)S(1)}, u32[]{:S(2)}, u32[]{:S(2)}) collective-permute-start(bf16[64,2048]{1,0:T(8,128)(2,1)S(1)} %get-tuple-element.69.n0), channel_id=1, source_target_pairs={{0,3},{1,0},{2,1},{3,2},{4,7},{5,4},{6,5},{7,6},{8,11},{9,8},{10,9... | collective-permute-start | bytes 786440 | tf_op jit(solution)/shard_map/ppermute | solution.py:44
  97.0 10.4 %collective-permute-start.13 = (bf16[64,2048]{1,0:T(8,128)(2,1)S(1)}, bf16[64,2048]{1,0:T(8,128)(2,1)S(1)}, u32[]{:S(2)}, u32[]{:S(2)}) collective-permute-start(bf16[64,2048]{1,0:T(8,128)(2,1)S(1)} %get-tuple-element.69.n0), channel_id=1, source_target_pairs={{0,2},{1,3},{2,0},{3,1},{4,6},{5,7},{6,4},{7,5},{8,10},{9,11},{10,... | collective-permute-start | bytes 786440 | tf_op jit(solution)/shard_map/ppermute | solution.py:44
  97.1 14.7 %collective-permute-start.14 = (bf16[64,2048]{1,0:T(8,128)(2,1)S(1)}, bf16[64,2048]{1,0:T(8,128)(2,1)S(1)}, u32[]{:S(2)}, u32[]{:S(2)}) collective-permute-start(bf16[64,2048]{1,0:T(8,128)(2,1)S(1)} %get-tuple-element.69.n0), channel_id=1, source_target_pairs={{0,1},{1,2},{2,3},{3,0},{4,5},{5,6},{6,7},{7,4},{8,9},{9,10},{10,1... | collective-permute-start | bytes 786440 | tf_op jit(solution)/shard_map/ppermute | solution.py:44
  111.8 4.8 %copy-start.26 = (f32[256]{0:T(256)S(1)}, f32[256]{0:T(256)}, u32[]{:S(2)}) copy-start(f32[256]{0:T(256)} %param.28) | copy-start | bytes 3076
  111.8 4.8 %copy-start.28 = (s32[8,384]{1,0:T(8,128)S(1)}, s32[8,384]{1,0:T(8,128)}, u32[]{:S(2)}) copy-start(s32[8,384]{1,0:T(8,128)} %copy-done.27) | copy-start | bytes 36868
  114.0 10.1 %collective-permute-start.15 = (bf16[16,2048]{1,0:T(8,128)(2,1)S(1)}, bf16[16,2048]{1,0:T(8,128)(2,1)S(1)}, u32[]{:S(2)}, u32[]{:S(2)}) collective-permute-start(bf16[16,2048]{1,0:T(8,128)(2,1)S(1)} %ffn3.1.t0), channel_id=1, source_target_pairs={{0,1},{1,2},{2,3},{3,0},{4,5},{5,6},{6,7},{7,4},{8,9},{9,10},{10,1... | collective-permute-start | bytes 196616 | tf_op jit(solution)/shard_map/ppermute | solution.py:44
  114.0 10.1 %collective-permute-start.16 = (bf16[16,2048]{1,0:T(8,128)(2,1)S(1)}, bf16[16,2048]{1,0:T(8,128)(2,1)S(1)}, u32[]{:S(2)}, u32[]{:S(2)}) collective-permute-start(bf16[16,2048]{1,0:T(8,128)(2,1)S(1)} %ffn3.1.t0), channel_id=1, source_target_pairs={{0,2},{1,3},{2,0},{3,1},{4,6},{5,7},{6,4},{7,5},{8,10},{9,11},{10,... | collective-permute-start | bytes 196616 | tf_op jit(solution)/shard_map/ppermute | solution.py:44
  114.6 9.4 %collective-permute-start.17 = (bf16[16,2048]{1,0:T(8,128)(2,1)S(1)}, bf16[16,2048]{1,0:T(8,128)(2,1)S(1)}, u32[]{:S(2)}, u32[]{:S(2)}) collective-permute-start(bf16[16,2048]{1,0:T(8,128)(2,1)S(1)} %ffn3.1.t0), channel_id=1, source_target_pairs={{0,3},{1,0},{2,1},{3,2},{4,7},{5,4},{6,5},{7,6},{8,11},{9,8},{10,9... | collective-permute-start | bytes 196616 | tf_op jit(solution)/shard_map/ppermute | solution.py:44
  116.7 1.2 copy-start.19
  117.9 9.3 %copy-start.14 = (f32[256]{0:T(256)S(1)}, f32[256]{0:T(256)}, u32[]{:S(2)}) copy-start(f32[256]{0:T(256)} %param.29) | copy-start | bytes 3076
  117.9 9.3 %copy-start.15 = (s32[4]{0:T(128)S(1)}, s32[4]{0:T(128)}, u32[]{:S(2)}) copy-start(s32[4]{0:T(128)} %counts.1) | copy-start | bytes 52
  124.7 2.5 %collective-permute-start.18 = (bf16[16,2048]{1,0:T(8,128)(2,1)}, bf16[16,2048]{1,0:T(8,128)(2,1)S(1)}, u32[]{:S(2)}, u32[]{:S(2)}) collective-permute-start(bf16[16,2048]{1,0:T(8,128)(2,1)} %pool.1), channel_id=1, source_target_pairs={{0,128},{128,0},{1,129},{129,1},{2,130},{130,2},{3,131},{131,3},{4... | collective-permute-start | bytes 196616 | tf_op jit(solution)/shard_map/ppermute | solution.py:50
  (2 other events, 1.2 us)
where the time goes:
time: 130 us; the launch traced here: 129 us
  starting transfers between devices  42 us (32%)
  waiting for transfers between devices  38 us (29%)
  Pallas kernels  32.9 us (25%)
  local copies, waits for them, and re-layouts  15.5 us (12%)
    ppermute x18, waiting for transfers between devices, shift(): lax.ppermute(value, axis, [(i, (i + by) % size) for i in range(size)])  34.3 us
    ppermute x18, starting transfers between devices, shift(): lax.ppermute(value, axis, [(i, (i + by) % size) for i in range(size)])  22.9 us
    unnamed x58, local copies, waits for them, and re-layouts  15.5 us
    all_to_all x1, starting transfers between devices, body(): lax.all_to_all(outgoing, 'dp', split_axis=0, concat_axis=0, tiled=True)  11.3 us
    all_to_all x1, starting transfers between devices, body(): lax.all_to_all(served, 'dp', split_axis=0, concat_axis=0, tiled=True)  6.36 us
    pallas_call x1, Pallas kernels, body(): call(rank_kernel, 'rank', (shape((rank_rows, CMAX, columns - ATT), F32),...  6.13 us
    pallas_call x1, Pallas kernels, body(): call(functools.partial(serve_kernel, group=4), 'serve', shape((owner_coun...  4.33 us
    pallas_call x1, Pallas kernels, body(): call(second_kernel, 'ffn1', quarter + (shape((own, width), BF),), [VMEM]...  3.73 us
  transfers between devices with their start and end apart: 21, of which 10 were waited for; matrix products, arithmetic and copies ran while one was open for 0% of the time, Pallas kernels for 14%

commit v1 on v0

--- a/solution.py
+++ b/solution.py
@@ -135,21 +135,30 @@
 
 
 def gathered(blocks, normed_s):
-    own = blocks[0].shape[0]
-    for k, ref in enumerate(blocks):
-        normed_s[k * own : (k + 1) * own, :] = ref[...]
+    first = 0
+    for ref in blocks:
+        normed_s[first : first + ref.shape[0], :] = ref[...]
+        first += ref.shape[0]
     return normed_s[...]
 
 
-def third_kernel(n0, n1, n2, n3, up, down, o0, o1, o2, o3, act_s, normed_s):
-    raise_rows(gathered((n0, n1, n2, n3), normed_s), up, act_s)
+def third_kernel(*refs):
+    *blocks, up, down, o0, o1, o2, o3, act_s, normed_s = refs
+    raise_rows(gathered(blocks, normed_s), up, act_s)
     lower(act_s, down, (o0, o1, o2, o3))
 
 
-def last_kernel(n0, n1, n2, n3, pool, base, up, down, out, act_s, normed_s):
-    raise_rows(gathered((n0, n1, n2, n3), normed_s), up, act_s)
+def last_kernel(*refs):
+    *blocks, pool, base, up, down, out, act_s, normed_s = refs
+    raise_rows(gathered(blocks, normed_s), up, act_s)
     mixed = dot(pool[...], act_s[...]).astype(BF)
     out[...] = (dot(mixed, down[...]) + base[...]).astype(BF)
+
+
+def halves_kernel(before, behind, top, bottom):
+    rows = top.shape[0]
+    top[...] = before[:rows, :]
+    bottom[...] = behind[rows:, :]
 
 
 def advance(t0, t1, t2, t3, state, chosen, code_rows):
@@ -284,9 +293,7 @@
             out[g + k] = found[k * capacity : (k + 1) * capacity, :]
 
 
-def rank_kernel(target, returned, bias, user_proj, out, user_proj_v, sem):
-    copy = pltpu.make_async_copy(user_proj, user_proj_v, sem)
-    copy.start()
+def rank_kernel(target, returned, bias, out, *, first):
     requests = out.shape[0]
     count, capacity, width = returned.shape
     table = returned[...].reshape(count * capacity, width)
@@ -294,26 +301,29 @@
     slots = targets.shape[0]
     ids = lax.broadcasted_iota(jnp.int32, (slots, count * capacity), 1)
     for q in range(requests):
-        rows = dot((targets[:, q : q + 1] == ids).astype(BF), table).astype(BF)
+        mine = targets[:, first + q : first + q + 1]
+        rows = dot((mine == ids).astype(BF), table).astype(BF)
         queries = rows[:CMAX, :ATT]
         keys = rows[CMAX:, :ATT]
         scores = lax.dot_general(queries, keys, NT, preferred_element_type=F32) / math.sqrt(ATT)
         weights = jax.nn.sigmoid(scores).astype(BF)
         interest = dot(weights, rows[CMAX:, ATT:]) / math.sqrt(HIST)
-        out[q] = interest + rows[:CMAX, ATT:].astype(F32) + bias[...]
-    copy.wait()
-
-
-def logit_kernel(counts, users, user_proj, units, weight, out, term_s):
-    term_s[...] = dot(users[...], user_proj[...])
-    requests = units.shape[0]
+        out[q] = jnp.transpose(interest + rows[:CMAX, ATT:].astype(F32) + bias[...])
+
+
+def logit_kernel(counts, users, user_proj, units0, units1, weight, out):
+    half, values, _ = units0.shape
+    requests = out.shape[0]
+    terms = jnp.transpose(dot(users[...], user_proj[...]))
     base = lax.axis_index("mp") * requests
+    rows = lax.broadcasted_iota(jnp.int32, terms.shape, 1)
     lanes = lax.broadcasted_iota(jnp.int32, (1, CMAX), 1)
+    scale = jnp.transpose(jnp.broadcast_to(weight[...], (8, values)))[:, :1]
     for q in range(requests):
-        hidden = jnp.maximum(units[q] + term_s[pl.ds(base + q, 1), :], 0.0)
-        line = lax.dot_general(
-            weight[...], hidden, NT, preferred_element_type=F32, precision=lax.Precision.HIGHEST
-        )
+        term = jnp.sum(jnp.where(rows == base + q, terms, 0.0), axis=1, keepdims=True)
+        unit = units0[q] if q < half else units1[q - half]
+        hidden = jnp.maximum(unit + term, 0.0) * scale
+        line = jnp.sum(hidden, axis=0, keepdims=True)
         out[q : q + 1, :] = jnp.where(lanes < counts[q], line, 0.0)
 
 
@@ -382,6 +392,16 @@
     )(beam_code, after(beam_parent, part), code_table)
     ffn = dict(limit=16, flops=4 * rows * width * hidden, moved=50 * width * hidden)
 
+    def shared(normed, ringed):
+        if not ringed:
+            return [normed] + [shift(normed, "mp", -k) for k in (1, 2, 3)]
+        behind, before = shift(normed, "mp", -1), shift(normed, "mp", 1)
+        top, bottom = call(
+            halves_kernel, "halves", (shape((own // 2, width), BF),) * 2, [VMEM] * 2, (VMEM,) * 2,
+            limit=16, flops=1000, moved=1_000_000,
+        )(before, behind)
+        return [normed, behind, shift(top, "mp", 1), shift(bottom, "mp", -1), before]
+
     quarter = (shape((own, width), BF),) * 4
     *outs, state = call(
         second_kernel, "ffn1", quarter + (shape((own, width), BF),),
@@ -403,9 +423,9 @@
         [HBM] * 2, (VMEM,) * 2, (DMA((2,)),), limit=40, flops=20 * rows * width * hidden, moved=1_000_000,
     )(after(up_weight, normed), after(down_weight, normed))
     wanted = after(wanted, normed)
-    others = [normed] + [shift(normed, "mp", -k) for k in (1, 2, 3)]
+    others = shared(normed, False)
     outs = call(
-        third_kernel, "ffn2", quarter, [VMEM] * 6, (VMEM,) * 4,
+        third_kernel, "ffn2", quarter, [VMEM] * (len(others) + 2), (VMEM,) * 4,
         (pltpu.VMEM((rows, hidden), BF), pltpu.VMEM((rows, width), BF)),
         **ffn,
     )(*others, up, down)
@@ -416,9 +436,9 @@
         limit=16, flops=2 * own * own * width, moved=2_000_000,
     )(*sums, state, chosen2, rows2, gain, pool, mean_code)
 
-    others = [normed] + [shift(normed, "mp", -k) for k in (1, 2, 3)]
+    others = shared(normed, False)
     part = call(
-        last_kernel, "ffn3", shape((requests, width), BF), [VMEM] * 8, VMEM,
+        last_kernel, "ffn3", shape((requests, width), BF), [VMEM] * (len(others) + 4), VMEM,
         (pltpu.VMEM((rows, hidden), BF), pltpu.VMEM((rows, width), BF)),
         **ffn,
     )(*others, pool, base, up, down)
@@ -434,24 +454,26 @@
     )(wanted, table)
     returned = lax.all_to_all(served, "dp", split_axis=0, concat_axis=0, tiled=True)
     returned = after(returned, part)
-    units, user_proj = call(
-        rank_kernel, "rank",
-        (shape((rank_rows, CMAX, columns - ATT), F32), shape(user_proj.shape, BF)),
-        [VMEM] * 3 + [HBM], (VMEM,) * 2, (DMA,), limit=16,
-        flops=2 * rank_rows * slots * owner_count * capacity * columns, moved=4_000_000,
-    )(target, returned, rank_bias.reshape(1, -1), user_proj)
-    part_late = after(part, units)
+    def ranked(first, count, blocks):
+        return call(
+            functools.partial(rank_kernel, first=first), f"rank{first}",
+            shape((count, columns - ATT, CMAX), F32), [VMEM] * 3, VMEM, limit=16,
+            flops=2 * count * slots * owner_count * capacity * columns, moved=4_000_000,
+        )(target, blocks, rank_bias.reshape(1, -1))
+
+    early = rank_rows // 2
+    units = [ranked(0, early, returned)]
     pooled = call(
         pool_kernel, "pool", shape((requests, width), BF), [VMEM] * 4, VMEM,
         limit=16, flops=100_000, moved=400_000,
-    )(part_late, *parts)
+    )(after(part, units[0]), *parts)
     partner = swapped(pooled, "section", 0)
+    units.append(ranked(early, rank_rows - early, after(returned, pooled)))
 
     logits = call(
-        logit_kernel, "logit", shape((rank_rows, CMAX), F32), [SMEM] + [VMEM] * 4, VMEM,
-        (pltpu.VMEM((requests, user_proj.shape[1]), F32),),
+        logit_kernel, "logit", shape((rank_rows, CMAX), F32), [SMEM] + [VMEM] * 5, VMEM,
         limit=16, flops=20_000_000, moved=1_600_000,
-    )(cand_count, partner, user_proj, units, out_weight.reshape(1, -1))
+    )(cand_count, partner, user_proj, *units, out_weight.reshape(1, -1))
     return (logits, pooled)
 
 

time: 130 us -> 128 us (0.985)
    pallas_call x3 -> x4, Pallas kernels: 10.8 us -> 11.4 us  [the longest x2 6.74 us: ranked(): call(functools.partial(rank_kernel, first=first), f'rank{first}', shape((...]
  transfers between devices with their start and end apart: 21 -> 21, of which waited for: 10 -> 9; matrix products, arithmetic and copies ran while one was open for 0% -> 0% of each run, Pallas kernels for 14% -> 15%
where the time goes in v1:
time: 128 us
  starting transfers between devices  42 us (33%)
  waiting for transfers between devices  37.2 us (29%)
  Pallas kernels  33.1 us (26%)
  local copies, waits for them, and re-layouts  14.3 us (11%)
    ppermute x18, waiting for transfers between devices, shift(): lax.ppermute(value, axis, [(i, (i + by) % size) for i in range(size)])  34.3 us
    ppermute x18, starting transfers between devices, shift(): lax.ppermute(value, axis, [(i, (i + by) % size) for i in range(size)])  22.9 us
    unnamed x58, local copies, waits for them, and re-layouts  14.3 us
    all_to_all x1, starting transfers between devices, body(): lax.all_to_all(outgoing, 'dp', split_axis=0, concat_axis=0, tiled=True)  11.3 us
    pallas_call x2, Pallas kernels, ranked(): call(functools.partial(rank_kernel, first=first), f'rank{first}', shape((...  6.74 us
    all_to_all x1, starting transfers between devices, body(): lax.all_to_all(served, 'dp', split_axis=0, concat_axis=0, tiled=True)  6.05 us
    pallas_call x1, Pallas kernels, body(): call(functools.partial(serve_kernel, group=4), 'serve', shape((owner_coun...  4.33 us
    pallas_call x1, Pallas kernels, body(): call(second_kernel, 'ffn1', quarter + (shape((own, width), BF),), [VMEM]...  3.76 us
  transfers between devices with their start and end apart: 21, of which 9 were waited for; matrix products, arithmetic and copies ran while one was open for 0% of the time, Pallas kernels for 15%

profile of v1, /device:TPU:1, one launch (start us, length us, event | category | flops | bytes accessed | tf_op | source)
XLA Modules:
  0.0 127.6 jit_solution(13357280572085619754)
XLA Ops:
  0.6 2.2 %copy-done.17 = bf16[2048,1024]{1,0:T(8,128)(2,1)S(1)} copy-done((bf16[2048,1024]{1,0:T(8,128)(2,1)S(1)}, bf16[2048,1024]{1,0:T(8,128)(2,1)}, u32[]{:S(2)}) %copy-start.17) | copy-done | bytes 4194328
  2.8 0.8 copy-done.20
  3.7 0.7 copy-done.23
  4.4 0.7 copy-done.24
  5.1 0.7 copy-done.25
  5.8 3.3 %start.1 = (s32[32,96]{1,0:T(8,128)S(1)}, s32[8,384]{1,0:T(8,128)S(1)}, bf16[16,2048]{1,0:T(8,128)(2,1)S(1)}, bf16[16,2048]{1,0:T(8,128)(2,1)S(1)}, f32[1,2048]{...) custom-call(s32[4,1,384]{2,1,0:T(1,128)S(1)} %bitcast.11, s32[4,384]{1,0:T(4,128)S(1)} %copy-done.25, ...), custom_call_target="tpu_custom_call" | custom-call | flops 53687091200 | bytes 1000000 | tf_op jit(solution)/shard_map/start/pallas_call | solution.py:360
  10.2 2.1 %collective-permute-start = (bf16[16,2048]{1,0:T(8,128)(2,1)S(1)}, bf16[16,2048]{1,0:T(8,128)(2,1)S(1)}, u32[]{:S(2)}, u32[]{:S(2)}) collective-permute-start(bf16[16,2048]{1,0:T(8,128)(2,1)S(1)} %get-tuple-element.41.t0), channel_id=1, source_target_pairs={{0,1},{1,2},{2,3},{3,0},{4,5},{5,6},{6,7},{7,4},{8,9},{9,10},{10,1... | collective-permute-start | bytes 196616 | tf_op jit(solution)/shard_map/ppermute | solution.py:44
  12.4 2.6 %collective-permute-start.1 = (bf16[16,2048]{1,0:T(8,128)(2,1)S(1)}, bf16[16,2048]{1,0:T(8,128)(2,1)S(1)}, u32[]{:S(2)}, u32[]{:S(2)}) collective-permute-start(bf16[16,2048]{1,0:T(8,128)(2,1)S(1)} %get-tuple-element.41.t0), channel_id=1, source_target_pairs={{0,2},{1,3},{2,0},{3,1},{4,6},{5,7},{6,4},{7,5},{8,10},{9,11},{10,... | collective-permute-start | bytes 196616 | tf_op jit(solution)/shard_map/ppermute | solution.py:44
  15.0 1.1 collective-permute-start.2
  16.1 2.1 %prepare.1 = (bf16[256,2048]{1,0:T(8,128)(2,1)S(1)}, bf16[64,2048]{1,0:T(8,128)(2,1)S(1)}, bf16[64,2048]{1,0:T(8,128)(2,1)S(1)}, f32[16,2048]{1,0:T(8,128)S(1)},...) custom-call(s32[16,4,16]{2,1,0:T(4,128)S(1)} %copy-done.21, ...), custom_call_target="tpu_custom_call" | custom-call | flops 419430400 | bytes 3000000 | tf_op jit(solution)/shard_map/prepare/pallas_call | solution.py:379
  18.4 3.8 %ffn1.1 = (bf16[64,2048]{1,0:T(8,128)(2,1)S(1)}, bf16[64,2048]{1,0:T(8,128)(2,1)}, bf16[64,2048]{1,0:T(8,128)(2,1)}, bf16[64,2048]{1,0:T(8,128)(2,1)}, bf16[64,2048]{1,0:T(8,128)(2,1)S(1)}) custom-call(bf16[16,2048]{1,0:T(8,128)(2,1)S(1)} %get-tuple-element.40.prompt, bf16[16,2048]{1,0:T(8,128)(2,1)S(1)} %get-tuple-element.41.t0, ...), custom_call_target="tpu_custom_call" | custom-call | flops 2147483648 | bytes 104857600 | tf_op jit(solution)/shard_map/ffn1/pallas_call | solution.py:406
  22.2 0.7 copy-done.6
  23.2 2.9 %collective-permute-start.4 = (bf16[64,2048]{1,0:T(8,128)(2,1)}, bf16[64,2048]{1,0:T(8,128)(2,1)}, u32[]{:S(2)}, u32[]{:S(2)}) collective-permute-start(bf16[64,2048]{1,0:T(8,128)(2,1)} %get-tuple-element.49), channel_id=1, source_target_pairs={{0,2},{1,3},{2,0},{3,1},{4,6},{5,7},{6,4},{7,5},{8,10},{9,11},{10,... | collective-permute-start | bytes 786440 | tf_op jit(solution)/shard_map/ppermute | solution.py:44
  26.2 11.3 %all-to-all-start = ((s32[32,1,96]{2,1,0:T(1,128)}), s32[32,1,96]{2,1,0:T(1,128)}, u32[]{:S(2)}, u32[]{:S(2)}) async-start(s32[32,1,96]{2,1,0:T(1,128)} %bitcast.8), calls=%async_computation | async-start | bytes 32768 | tf_op jit(solution)/shard_map/all_to_all | solution.py:414
  37.5 1.2 table.3
  38.8 0.9 copy-done.4
  39.7 0.9 copy-done.7
  40.7 0.7 copy-done.13
  41.4 1.6 %owner1.1 = (bf16[64,2048]{1,0:T(8,128)(2,1)S(1)}, bf16[64,2048]{1,0:T(8,128)(2,1)S(1)}) custom-call(bf16[64,2048]{1,0:T(8,128)(2,1)S(1)} %get-tuple-element.47.t0, bf16[64,2048]{1,0:T(8,128)(2,1)} %collective-permute-done.3.t1, bf16[64,2048]{1,0:T(8,128)(2,1)} %collective-permute-done.4.t2, bf16[64,2048]{1,0:T(8,128)(2,1)} %collective-permute-done.5.t3, ...), custom_call_target="tpu_custom_call" | custom-call | flops 16777216 | bytes 2000000 | tf_op jit(solution)/shard_map/owner1/pallas_call | solution.py:416
  43.0 2.9 %all-to-all-done = s32[32,1,96]{2,1,0:T(1,128)} async-done(((s32[32,1,96]{2,1,0:T(1,128)}), s32[32,1,96]{2,1,0:T(1,128)}, u32[]{:S(2)}, u32[]{:S(2)}) %all-to-all-start) | async-done | bytes 12320 | tf_op jit(solution)/shard_map/all_to_all | solution.py:414
  45.9 1.1 copy-done.5
  47.0 4.3 %serve.1 = bf16[32,96,384]{2,1,0:T(8,128)(2,1)S(1)} custom-call(s32[32,96]{1,0:T(8,128)} %bitcast.4.wanted, bf16[1024,384]{1,0:T(8,128)(2,1)S(1)} %copy-done.5), custom_call_target="tpu_custom_call" | custom-call | flops 2415919104 | bytes 4000000 | tf_op jit(solution)/shard_map/serve/pallas_call | solution.py:450
  51.4 1.4 %copy-done = bf16[32,96,384]{2,1,0:T(8,128)(2,1)} copy-done((bf16[32,96,384]{2,1,0:T(8,128)(2,1)}, bf16[32,96,384]{2,1,0:T(8,128)(2,1)S(1)}, u32[]{:S(2)}) %copy-start) | copy-done | bytes 2359320
  52.8 6.1 %all-to-all-start.1 = ((bf16[32,96,384]{2,1,0:T(8,128)(2,1)}), bf16[32,96,384]{2,1,0:T(8,128)(2,1)S(1)}, u32[]{:S(2)}, u32[]{:S(2)}) async-start(bf16[32,96,384]{2,1,0:T(8,128)(2,1)} %copy-done), calls=%async_computation.1 | async-start | bytes 4718592 | tf_op jit(solution)/shard_map/all_to_all | solution.py:455
  58.8 3.3 %collective-permute-start.6 = (bf16[64,2048]{1,0:T(8,128)(2,1)S(1)}, bf16[64,2048]{1,0:T(8,128)(2,1)S(1)}, u32[]{:S(2)}, u32[]{:S(2)}) collective-permute-start(bf16[64,2048]{1,0:T(8,128)(2,1)S(1)} %get-tuple-element.54.refs_0_), channel_id=1, source_target_pairs={{0,3},{1,0},{2,1},{3,2},{4,7},{5,4},{6,5},{7,6},{8,11},{9,8},{10,9... | collective-permute-start | bytes 786440 | tf_op jit(solution)/shard_map/ppermute | solution.py:44
  62.2 0.7 collective-permute-start.8
  62.8 2.2 %copy-done.18 = bf16[2048,1024]{1,0:T(8,128)(2,1)S(1)} copy-done((bf16[2048,1024]{1,0:T(8,128)(2,1)S(1)}, bf16[2048,1024]{1,0:T(8,128)(2,1)}, u32[]{:S(2)}) %copy-start.18) | copy-done | bytes 4194328
  65.0 2.5 %load.1 = (bf16[2048,1024]{1,0:T(8,128)(2,1)S(1)}, bf16[1024,2048]{1,0:T(8,128)(2,1)S(1)}) custom-call(bf16[2048,1024]{1,0:T(8,128)(2,1)S(1)} %copy-done.18, bf16[1024,2048]{1,0:T(8,128)(2,1)} %down.2), custom_call_target="tpu_custom_call" | custom-call | flops 10737418240 | bytes 1000000 | tf_op jit(solution)/shard_map/load/pallas_call | solution.py:421
  67.5 5.3 %collective-permute-done.6.refs_1_ = bf16[64,2048]{1,0:T(8,128)(2,1)S(1)} collective-permute-done((bf16[64,2048]{1,0:T(8,128)(2,1)S(1)}, bf16[64,2048]{1,0:T(8,128)(2,1)S(1)}, u32[]{:S(2)}, u32[]{:S(2)}) %collective-permute-start.6) | collective-permute-done | bytes 262176 | tf_op jit(solution)/shard_map/ppermute | solution.py:44
  72.8 3.7 %collective-permute-done.8.refs_3_ = bf16[64,2048]{1,0:T(8,128)(2,1)S(1)} collective-permute-done((bf16[64,2048]{1,0:T(8,128)(2,1)S(1)}, bf16[64,2048]{1,0:T(8,128)(2,1)S(1)}, u32[]{:S(2)}, u32[]{:S(2)}) %collective-permute-start.8) | collective-permute-done | bytes 262176 | tf_op jit(solution)/shard_map/ppermute | solution.py:44
  76.5 2.5 %ffn2.1 = (bf16[64,2048]{1,0:T(8,128)(2,1)S(1)}, bf16[64,2048]{1,0:T(8,128)(2,1)S(1)}, bf16[64,2048]{1,0:T(8,128)(2,1)S(1)}, bf16[64,2048]{1,0:T(8,128)(2,1)S(1)}) custom-call(bf16[64,2048]{1,0:T(8,128)(2,1)S(1)} %get-tuple-element.54.refs_0_, bf16[64,2048]{1,0:T(8,128)(2,1)S(1)} %collective-permute-done.6.refs_1_, ...), custom_call_target="tpu_custom_call" | custom-call | flops 2147483648 | bytes 104857600 | tf_op jit(solution)/shard_map/ffn2/pallas_call | solution.py:427
  79.1 1.1 collective-permute-start.10
  80.2 1.6 %collective-permute-start.11 = (bf16[64,2048]{1,0:T(8,128)(2,1)S(1)}, bf16[64,2048]{1,0:T(8,128)(2,1)S(1)}, u32[]{:S(2)}, u32[]{:S(2)}) collective-permute-start(bf16[64,2048]{1,0:T(8,128)(2,1)S(1)} %get-tuple-element.62), channel_id=1, source_target_pairs={{0,3},{1,0},{2,1},{3,2},{4,7},{5,4},{6,5},{7,6},{8,11},{9,8},{10,9... | collective-permute-start | bytes 786440 | tf_op jit(solution)/shard_map/ppermute | solution.py:44
  81.8 7.6 %collective-permute-done.9.t1 = bf16[64,2048]{1,0:T(8,128)(2,1)S(1)} collective-permute-done((bf16[64,2048]{1,0:T(8,128)(2,1)S(1)}, bf16[64,2048]{1,0:T(8,128)(2,1)S(1)}, u32[]{:S(2)}, u32[]{:S(2)}) %collective-permute-start.9) | collective-permute-done | bytes 262176 | tf_op jit(solution)/shard_map/ppermute | solution.py:44
  89.3 0.8 collective-permute-done.10.t2
  90.2 2.9 %collective-permute-done.11.t3 = bf16[64,2048]{1,0:T(8,128)(2,1)S(1)} collective-permute-done((bf16[64,2048]{1,0:T(8,128)(2,1)S(1)}, bf16[64,2048]{1,0:T(8,128)(2,1)S(1)}, u32[]{:S(2)}, u32[]{:S(2)}) %collective-permute-start.11) | collective-permute-done | bytes 262176 | tf_op jit(solution)/shard_map/ppermute | solution.py:44
  93.6 3.5 %collective-permute-start.12 = (bf16[64,2048]{1,0:T(8,128)(2,1)S(1)}, bf16[64,2048]{1,0:T(8,128)(2,1)S(1)}, u32[]{:S(2)}, u32[]{:S(2)}) collective-permute-start(bf16[64,2048]{1,0:T(8,128)(2,1)S(1)} %get-tuple-element.68.refs_0_), channel_id=1, source_target_pairs={{0,3},{1,0},{2,1},{3,2},{4,7},{5,4},{6,5},{7,6},{8,11},{9,8},{10,9... | collective-permute-start | bytes 786440 | tf_op jit(solution)/shard_map/ppermute | solution.py:44
  97.1 0.9 collective-permute-start.14
  98.0 9.5 %collective-permute-done.12.refs_1_ = bf16[64,2048]{1,0:T(8,128)(2,1)S(1)} collective-permute-done((bf16[64,2048]{1,0:T(8,128)(2,1)S(1)}, bf16[64,2048]{1,0:T(8,128)(2,1)S(1)}, u32[]{:S(2)}, u32[]{:S(2)}) %collective-permute-start.12) | collective-permute-done | bytes 262176 | tf_op jit(solution)/shard_map/ppermute | solution.py:44
  107.4 4.4 %collective-permute-done.14.refs_3_ = bf16[64,2048]{1,0:T(8,128)(2,1)S(1)} collective-permute-done((bf16[64,2048]{1,0:T(8,128)(2,1)S(1)}, bf16[64,2048]{1,0:T(8,128)(2,1)S(1)}, u32[]{:S(2)}, u32[]{:S(2)}) %collective-permute-start.14) | collective-permute-done | bytes 262176 | tf_op jit(solution)/shard_map/ppermute | solution.py:44
  111.8 2.1 %ffn3.1.t0 = bf16[16,2048]{1,0:T(8,128)(2,1)S(1)} custom-call(bf16[64,2048]{1,0:T(8,128)(2,1)S(1)} %get-tuple-element.68.refs_0_, bf16[64,2048]{1,0:T(8,128)(2,1)S(1)} %collective-permute-done.12.refs_1_, bf16[64,2048]{1,0:T(8,128)(2,1)S(1)} %collective-permute-done.13.refs_2_, bf16[64,2048]{1,0:T(8,128)(2,1)S(1)} %collective-permute-done.14.refs_3_, ...), custom_call_target="tpu_custom_call" | custom-call | flops 2147483648 | bytes 104857600 | tf_op jit(solution)/shard_map/ffn3/pallas_call | solution.py:440
  114.0 0.7 collective-permute-start.16
  114.7 2.0 %collective-permute-start.17 = (bf16[16,2048]{1,0:T(8,128)(2,1)S(1)}, bf16[16,2048]{1,0:T(8,128)(2,1)S(1)}, u32[]{:S(2)}, u32[]{:S(2)}) collective-permute-start(bf16[16,2048]{1,0:T(8,128)(2,1)S(1)} %ffn3.1.t0), channel_id=1, source_target_pairs={{0,3},{1,0},{2,1},{3,2},{4,7},{5,4},{6,5},{7,6},{8,11},{9,8},{10,9... | collective-permute-start | bytes 196616 | tf_op jit(solution)/shard_map/ppermute | solution.py:44
  116.7 3.4 %rank0.1.units0 = f32[2,256,128]{2,1,0:T(8,128)S(1)} custom-call(s32[8,384]{1,0:T(8,128)S(1)} %copy-done.28, bf16[32,96,384]{2,1,0:T(8,128)(2,1)S(1)} %all-to-all-done.1.returned, f32[1,256]{1,0:T(1,128)S(1)} %bitcast.12), custom_call_target="tpu_custom_call" | custom-call | flops 1811939328 | bytes 4000000 | tf_op jit(solution)/shard_map/rank0/pallas_call | solution.py:458
  120.1 0.7 pool.1
  120.8 1.7 %collective-permute-start.18 = (bf16[16,2048]{1,0:T(8,128)(2,1)}, bf16[16,2048]{1,0:T(8,128)(2,1)S(1)}, u32[]{:S(2)}, u32[]{:S(2)}) collective-permute-start(bf16[16,2048]{1,0:T(8,128)(2,1)} %pool.1), channel_id=1, source_target_pairs={{0,128},{128,0},{1,129},{129,1},{2,130},{130,2},{3,131},{131,3},{4... | collective-permute-start | bytes 196616 | tf_op jit(solution)/shard_map/ppermute | solution.py:50
  122.5 3.4 %rank2.1.units1 = f32[2,256,128]{2,1,0:T(8,128)S(1)} custom-call(s32[8,384]{1,0:T(8,128)S(1)} %copy-done.28, bf16[32,96,384]{2,1,0:T(8,128)(2,1)S(1)} %all-to-all-done.1.returned, f32[1,256]{1,0:T(1,128)S(1)} %bitcast.13), custom_call_target="tpu_custom_call" | custom-call | flops 1811939328 | bytes 4000000 | tf_op jit(solution)/shard_map/rank2/pallas_call | solution.py:458
  125.9 1.7 %logit.1 = f32[4,128]{1,0:T(4,128)} custom-call(s32[4]{0:T(128)S(1)} %copy-done.16, bf16[16,2048]{1,0:T(8,128)(2,1)S(1)} %collective-permute-done.18.users, bf16[2048,256]{1,0:T(8,128)(2,1)S(1)} %copy-done.2, f32[2,256,128]{2,1,0:T(8,128)S(1)} %rank0.1.units0, f32[2,256,128]{2,1,0:T(8,128)S(1)} %rank2.1.units1, f32[1,256]{1,0:T(1,128)S(1)} %bitcast.9), custom_call_target="tpu_custom_call" | custom-call | flops 20000000 | bytes 1600000 | tf_op jit(solution)/shard_map/logit/pallas_call | solution.py:473
  (66 shorter events, 2.5 us)
Async XLA Ops:
  0.6 2.2 %copy-start.17 = (bf16[2048,1024]{1,0:T(8,128)(2,1)S(1)}, bf16[2048,1024]{1,0:T(8,128)(2,1)}, u32[]{:S(2)}) copy-start(bf16[2048,1024]{1,0:T(8,128)(2,1)} %up.2) | copy-start | bytes 12582916
  2.8 0.8 copy-start.20
  3.7 0.7 copy-start.23
  4.4 0.7 copy-start.24
  5.1 0.7 copy-start.25
  5.7 10.3 %copy-start.19 = (bf16[256,2048]{1,0:T(8,128)(2,1)S(1)}, bf16[256,2048]{1,0:T(8,128)(2,1)}, u32[]{:S(2)}) copy-start(bf16[256,2048]{1,0:T(8,128)(2,1)} %table.2) | copy-start | bytes 3145732
  5.7 10.3 %copy-start.21 = (s32[16,4,16]{2,1,0:T(4,128)S(1)}, s32[16,4,16]{2,1,0:T(4,128)}, u32[]{:S(2)}) copy-start(s32[16,4,16]{2,1,0:T(4,128)} %code.1) | copy-start | bytes 12292
  5.7 10.3 %copy-start.22 = (s32[16,4,16]{2,1,0:T(4,128)S(1)}, s32[16,4,16]{2,1,0:T(4,128)}, u32[]{:S(2)}) copy-start(s32[16,4,16]{2,1,0:T(4,128)} %parent) | copy-start | bytes 12292
  10.2 8.0 %collective-permute-start = (bf16[16,2048]{1,0:T(8,128)(2,1)S(1)}, bf16[16,2048]{1,0:T(8,128)(2,1)S(1)}, u32[]{:S(2)}, u32[]{:S(2)}) collective-permute-start(bf16[16,2048]{1,0:T(8,128)(2,1)S(1)} %get-tuple-element.41.t0), channel_id=1, source_target_pairs={{0,1},{1,2},{2,3},{3,0},{4,5},{5,6},{6,7},{7,4},{8,9},{9,10},{10,1... | collective-permute-start | bytes 196616 | tf_op jit(solution)/shard_map/ppermute | solution.py:44
  12.4 5.9 %collective-permute-start.1 = (bf16[16,2048]{1,0:T(8,128)(2,1)S(1)}, bf16[16,2048]{1,0:T(8,128)(2,1)S(1)}, u32[]{:S(2)}, u32[]{:S(2)}) collective-permute-start(bf16[16,2048]{1,0:T(8,128)(2,1)S(1)} %get-tuple-element.41.t0), channel_id=1, source_target_pairs={{0,2},{1,3},{2,0},{3,1},{4,6},{5,7},{6,4},{7,5},{8,10},{9,11},{10,... | collective-permute-start | bytes 196616 | tf_op jit(solution)/shard_map/ppermute | solution.py:44
  15.0 3.4 %collective-permute-start.2 = (bf16[16,2048]{1,0:T(8,128)(2,1)S(1)}, bf16[16,2048]{1,0:T(8,128)(2,1)S(1)}, u32[]{:S(2)}, u32[]{:S(2)}) collective-permute-start(bf16[16,2048]{1,0:T(8,128)(2,1)S(1)} %get-tuple-element.41.t0), channel_id=1, source_target_pairs={{0,3},{1,0},{2,1},{3,2},{4,7},{5,4},{6,5},{7,6},{8,11},{9,8},{10,9... | collective-permute-start | bytes 196616 | tf_op jit(solution)/shard_map/ppermute | solution.py:44
  18.2 3.9 %copy-start.8 = (bf16[64,2048]{1,0:T(8,128)(2,1)}, bf16[64,2048]{1,0:T(8,128)(2,1)S(1)}, u32[]{:S(2)}) copy-start(bf16[64,2048]{1,0:T(8,128)(2,1)S(1)} %get-tuple-element.65.code_rows) | copy-start | bytes 786436
  18.2 3.9 %copy-start.10 = (bf16[64,64]{1,0:T(8,128)(2,1)}, bf16[64,64]{1,0:T(8,128)(2,1)S(1)}, u32[]{:S(2)}) copy-start(bf16[64,64]{1,0:T(8,128)(2,1)S(1)} %get-tuple-element.64.chosen) | copy-start | bytes 24580
  18.2 3.9 %copy-start.12 = (bf16[64,64]{1,0:T(8,128)(2,1)}, bf16[64,64]{1,0:T(8,128)(2,1)S(1)}, u32[]{:S(2)}) copy-start(bf16[64,64]{1,0:T(8,128)(2,1)S(1)} %get-tuple-element.52.chosen) | copy-start | bytes 24580
  18.4 19.1 %copy-start.1 = (bf16[1024,1024]{1,0:T(8,128)(2,1)S(1)}, bf16[1024,1024]{1,0:T(8,128)(2,1)}, u32[]{:S(2)}) copy-start(bf16[1024,1024]{1,0:T(8,128)(2,1)} %features.1) | copy-start | bytes 6291460
  18.4 19.1 %copy-start.3 = (bf16[1024,384]{1,0:T(8,128)(2,1)S(1)}, bf16[1024,384]{1,0:T(8,128)(2,1)}, u32[]{:S(2)}) copy-start(bf16[1024,384]{1,0:T(8,128)(2,1)} %proj) | copy-start | bytes 2359300
  22.2 0.7 copy-start.6
  22.9 16.8 %collective-permute-start.3 = (bf16[64,2048]{1,0:T(8,128)(2,1)}, bf16[64,2048]{1,0:T(8,128)(2,1)}, u32[]{:S(2)}, u32[]{:S(2)}) collective-permute-start(bf16[64,2048]{1,0:T(8,128)(2,1)} %get-tuple-element.48), channel_id=1, source_target_pairs={{0,1},{1,2},{2,3},{3,0},{4,5},{5,6},{6,7},{7,4},{8,9},{9,10},{10,1... | collective-permute-start | bytes 786440 | tf_op jit(solution)/shard_map/ppermute | solution.py:44
  23.2 16.5 %collective-permute-start.4 = (bf16[64,2048]{1,0:T(8,128)(2,1)}, bf16[64,2048]{1,0:T(8,128)(2,1)}, u32[]{:S(2)}, u32[]{:S(2)}) collective-permute-start(bf16[64,2048]{1,0:T(8,128)(2,1)} %get-tuple-element.49), channel_id=1, source_target_pairs={{0,2},{1,3},{2,0},{3,1},{4,6},{5,7},{6,4},{7,5},{8,10},{9,11},{10,... | collective-permute-start | bytes 786440 | tf_op jit(solution)/shard_map/ppermute | solution.py:44
  26.0 13.7 %collective-permute-start.5 = (bf16[64,2048]{1,0:T(8,128)(2,1)}, bf16[64,2048]{1,0:T(8,128)(2,1)}, u32[]{:S(2)}, u32[]{:S(2)}) collective-permute-start(bf16[64,2048]{1,0:T(8,128)(2,1)} %get-tuple-element.50), channel_id=1, source_target_pairs={{0,3},{1,0},{2,1},{3,2},{4,7},{5,4},{6,5},{7,6},{8,11},{9,8},{10,9... | collective-permute-start | bytes 786440 | tf_op jit(solution)/shard_map/ppermute | solution.py:44
  26.2 19.7 %all-to-all-start = ((s32[32,1,96]{2,1,0:T(1,128)}), s32[32,1,96]{2,1,0:T(1,128)}, u32[]{:S(2)}, u32[]{:S(2)}) async-start(s32[32,1,96]{2,1,0:T(1,128)} %bitcast.8), calls=%async_computation | async-start | bytes 32768 | tf_op jit(solution)/shard_map/all_to_all | solution.py:414
  38.8 0.9 copy-start.4
  39.7 1.0 copy-start.7
  40.7 0.7 copy-start.13
  45.9 1.1 copy-start.5
  51.4 1.4 %copy-start = (bf16[32,96,384]{2,1,0:T(8,128)(2,1)}, bf16[32,96,384]{2,1,0:T(8,128)(2,1)S(1)}, u32[]{:S(2)}) copy-start(bf16[32,96,384]{2,1,0:T(8,128)(2,1)S(1)} %serve.1) | copy-start | bytes 7077892
  52.8 63.9 %all-to-all-start.1 = ((bf16[32,96,384]{2,1,0:T(8,128)(2,1)}), bf16[32,96,384]{2,1,0:T(8,128)(2,1)S(1)}, u32[]{:S(2)}, u32[]{:S(2)}) async-start(bf16[32,96,384]{2,1,0:T(8,128)(2,1)} %copy-done), calls=%async_computation.1 | async-start | bytes 4718592 | tf_op jit(solution)/shard_map/all_to_all | solution.py:455
  58.8 13.9 %collective-permute-start.6 = (bf16[64,2048]{1,0:T(8,128)(2,1)S(1)}, bf16[64,2048]{1,0:T(8,128)(2,1)S(1)}, u32[]{:S(2)}, u32[]{:S(2)}) collective-permute-start(bf16[64,2048]{1,0:T(8,128)(2,1)S(1)} %get-tuple-element.54.refs_0_), channel_id=1, source_target_pairs={{0,3},{1,0},{2,1},{3,2},{4,7},{5,4},{6,5},{7,6},{8,11},{9,8},{10,9... | collective-permute-start | bytes 786440 | tf_op jit(solution)/shard_map/ppermute | solution.py:44
  62.1 10.7 %collective-permute-start.7 = (bf16[64,2048]{1,0:T(8,128)(2,1)S(1)}, bf16[64,2048]{1,0:T(8,128)(2,1)S(1)}, u32[]{:S(2)}, u32[]{:S(2)}) collective-permute-start(bf16[64,2048]{1,0:T(8,128)(2,1)S(1)} %get-tuple-element.54.refs_0_), channel_id=1, source_target_pairs={{0,2},{1,3},{2,0},{3,1},{4,6},{5,7},{6,4},{7,5},{8,10},{9,11},{10,... | collective-permute-start | bytes 786440 | tf_op jit(solution)/shard_map/ppermute | solution.py:44
  62.2 14.3 %collective-permute-start.8 = (bf16[64,2048]{1,0:T(8,128)(2,1)S(1)}, bf16[64,2048]{1,0:T(8,128)(2,1)S(1)}, u32[]{:S(2)}, u32[]{:S(2)}) collective-permute-start(bf16[64,2048]{1,0:T(8,128)(2,1)S(1)} %get-tuple-element.54.refs_0_), channel_id=1, source_target_pairs={{0,1},{1,2},{2,3},{3,0},{4,5},{5,6},{6,7},{7,4},{8,9},{9,10},{10,1... | collective-permute-start | bytes 786440 | tf_op jit(solution)/shard_map/ppermute | solution.py:44
  62.8 2.2 %copy-start.18 = (bf16[2048,1024]{1,0:T(8,128)(2,1)S(1)}, bf16[2048,1024]{1,0:T(8,128)(2,1)}, u32[]{:S(2)}) copy-start(bf16[2048,1024]{1,0:T(8,128)(2,1)} %up.2) | copy-start | bytes 12582916
  76.5 16.6 %copy-start.9 = (bf16[64,2048]{1,0:T(8,128)(2,1)S(1)}, bf16[64,2048]{1,0:T(8,128)(2,1)}, u32[]{:S(2)}) copy-start(bf16[64,2048]{1,0:T(8,128)(2,1)} %copy-done.8) | copy-start | bytes 786436
  76.5 16.6 %copy-start.11 = (bf16[64,64]{1,0:T(8,128)(2,1)S(1)}, bf16[64,64]{1,0:T(8,128)(2,1)}, u32[]{:S(2)}) copy-start(bf16[64,64]{1,0:T(8,128)(2,1)} %copy-done.10) | copy-start | bytes 24580
  79.0 10.3 %collective-permute-start.9 = (bf16[64,2048]{1,0:T(8,128)(2,1)S(1)}, bf16[64,2048]{1,0:T(8,128)(2,1)S(1)}, u32[]{:S(2)}, u32[]{:S(2)}) collective-permute-start(bf16[64,2048]{1,0:T(8,128)(2,1)S(1)} %get-tuple-element.60), channel_id=1, source_target_pairs={{0,1},{1,2},{2,3},{3,0},{4,5},{5,6},{6,7},{7,4},{8,9},{9,10},{10,1... | collective-permute-start | bytes 786440 | tf_op jit(solution)/shard_map/ppermute | solution.py:44
  79.1 11.1 %collective-permute-start.10 = (bf16[64,2048]{1,0:T(8,128)(2,1)S(1)}, bf16[64,2048]{1,0:T(8,128)(2,1)S(1)}, u32[]{:S(2)}, u32[]{:S(2)}) collective-permute-start(bf16[64,2048]{1,0:T(8,128)(2,1)S(1)} %get-tuple-element.61), channel_id=1, source_target_pairs={{0,2},{1,3},{2,0},{3,1},{4,6},{5,7},{6,4},{7,5},{8,10},{9,11},{10,... | collective-permute-start | bytes 786440 | tf_op jit(solution)/shard_map/ppermute | solution.py:44
  80.2 12.9 %collective-permute-start.11 = (bf16[64,2048]{1,0:T(8,128)(2,1)S(1)}, bf16[64,2048]{1,0:T(8,128)(2,1)S(1)}, u32[]{:S(2)}, u32[]{:S(2)}) collective-permute-start(bf16[64,2048]{1,0:T(8,128)(2,1)S(1)} %get-tuple-element.62), channel_id=1, source_target_pairs={{0,3},{1,0},{2,1},{3,2},{4,7},{5,4},{6,5},{7,6},{8,11},{9,8},{10,9... | collective-permute-start | bytes 786440 | tf_op jit(solution)/shard_map/ppermute | solution.py:44
  93.6 13.9 %collective-permute-start.12 = (bf16[64,2048]{1,0:T(8,128)(2,1)S(1)}, bf16[64,2048]{1,0:T(8,128)(2,1)S(1)}, u32[]{:S(2)}, u32[]{:S(2)}) collective-permute-start(bf16[64,2048]{1,0:T(8,128)(2,1)S(1)} %get-tuple-element.68.refs_0_), channel_id=1, source_target_pairs={{0,3},{1,0},{2,1},{3,2},{4,7},{5,4},{6,5},{7,6},{8,11},{9,8},{10,9... | collective-permute-start | bytes 786440 | tf_op jit(solution)/shard_map/ppermute | solution.py:44
  97.1 10.4 %collective-permute-start.13 = (bf16[64,2048]{1,0:T(8,128)(2,1)S(1)}, bf16[64,2048]{1,0:T(8,128)(2,1)S(1)}, u32[]{:S(2)}, u32[]{:S(2)}) collective-permute-start(bf16[64,2048]{1,0:T(8,128)(2,1)S(1)} %get-tuple-element.68.refs_0_), channel_id=1, source_target_pairs={{0,2},{1,3},{2,0},{3,1},{4,6},{5,7},{6,4},{7,5},{8,10},{9,11},{10,... | collective-permute-start | bytes 786440 | tf_op jit(solution)/shard_map/ppermute | solution.py:44
  97.1 14.7 %collective-permute-start.14 = (bf16[64,2048]{1,0:T(8,128)(2,1)S(1)}, bf16[64,2048]{1,0:T(8,128)(2,1)S(1)}, u32[]{:S(2)}, u32[]{:S(2)}) collective-permute-start(bf16[64,2048]{1,0:T(8,128)(2,1)S(1)} %get-tuple-element.68.refs_0_), channel_id=1, source_target_pairs={{0,1},{1,2},{2,3},{3,0},{4,5},{5,6},{6,7},{7,4},{8,9},{9,10},{10,1... | collective-permute-start | bytes 786440 | tf_op jit(solution)/shard_map/ppermute | solution.py:44
  111.8 4.8 %copy-start.26 = (f32[256]{0:T(256)S(1)}, f32[256]{0:T(256)}, u32[]{:S(2)}) copy-start(f32[256]{0:T(256)} %param.28) | copy-start | bytes 3076
  111.8 4.8 %copy-start.28 = (s32[8,384]{1,0:T(8,128)S(1)}, s32[8,384]{1,0:T(8,128)}, u32[]{:S(2)}) copy-start(s32[8,384]{1,0:T(8,128)} %copy-done.27) | copy-start | bytes 36868
  114.0 6.1 %collective-permute-start.15 = (bf16[16,2048]{1,0:T(8,128)(2,1)S(1)}, bf16[16,2048]{1,0:T(8,128)(2,1)S(1)}, u32[]{:S(2)}, u32[]{:S(2)}) collective-permute-start(bf16[16,2048]{1,0:T(8,128)(2,1)S(1)} %ffn3.1.t0), channel_id=1, source_target_pairs={{0,1},{1,2},{2,3},{3,0},{4,5},{5,6},{6,7},{7,4},{8,9},{9,10},{10,1... | collective-permute-start | bytes 196616 | tf_op jit(solution)/shard_map/ppermute | solution.py:44
  114.0 6.1 %collective-permute-start.16 = (bf16[16,2048]{1,0:T(8,128)(2,1)S(1)}, bf16[16,2048]{1,0:T(8,128)(2,1)S(1)}, u32[]{:S(2)}, u32[]{:S(2)}) collective-permute-start(bf16[16,2048]{1,0:T(8,128)(2,1)S(1)} %ffn3.1.t0), channel_id=1, source_target_pairs={{0,2},{1,3},{2,0},{3,1},{4,6},{5,7},{6,4},{7,5},{8,10},{9,11},{10,... | collective-permute-start | bytes 196616 | tf_op jit(solution)/shard_map/ppermute | solution.py:44
  114.7 5.4 %collective-permute-start.17 = (bf16[16,2048]{1,0:T(8,128)(2,1)S(1)}, bf16[16,2048]{1,0:T(8,128)(2,1)S(1)}, u32[]{:S(2)}, u32[]{:S(2)}) collective-permute-start(bf16[16,2048]{1,0:T(8,128)(2,1)S(1)} %ffn3.1.t0), channel_id=1, source_target_pairs={{0,3},{1,0},{2,1},{3,2},{4,7},{5,4},{6,5},{7,6},{8,11},{9,8},{10,9... | collective-permute-start | bytes 196616 | tf_op jit(solution)/shard_map/ppermute | solution.py:44
  120.1 5.8 %copy-start.2 = (bf16[2048,256]{1,0:T(8,128)(2,1)S(1)}, bf16[2048,256]{1,0:T(8,128)(2,1)}, u32[]{:S(2)}) copy-start(bf16[2048,256]{1,0:T(8,128)(2,1)} %user_proj.1) | copy-start | bytes 3145732
  120.1 5.8 %copy-start.15 = (f32[256]{0:T(256)S(1)}, f32[256]{0:T(256)}, u32[]{:S(2)}) copy-start(f32[256]{0:T(256)} %param.29) | copy-start | bytes 3076
  120.1 5.8 %copy-start.16 = (s32[4]{0:T(128)S(1)}, s32[4]{0:T(128)}, u32[]{:S(2)}) copy-start(s32[4]{0:T(128)} %counts.1) | copy-start | bytes 52
  120.8 5.1 %collective-permute-start.18 = (bf16[16,2048]{1,0:T(8,128)(2,1)}, bf16[16,2048]{1,0:T(8,128)(2,1)S(1)}, u32[]{:S(2)}, u32[]{:S(2)}) collective-permute-start(bf16[16,2048]{1,0:T(8,128)(2,1)} %pool.1), channel_id=1, source_target_pairs={{0,128},{128,0},{1,129},{129,1},{2,130},{130,2},{3,131},{131,3},{4... | collective-permute-start | bytes 196616 | tf_op jit(solution)/shard_map/ppermute | solution.py:50
  (2 other events, 1.2 us)

commit v2 on v1

--- a/solution.py
+++ b/solution.py
@@ -281,16 +281,22 @@
     table[...] = dot(features[...], proj[...]).astype(BF)
 
 
-def serve_kernel(wanted, table, out, *, group):
+def serve_kernel(wanted, table, out, found_s, sems, *, group):
     rows = table.shape[0]
     count, capacity, _ = out.shape
     asked = jnp.transpose(wanted[...])
     ids = lax.broadcasted_iota(jnp.int32, (capacity * group, rows), 1)
+    sends = []
     for g in range(0, count, group):
         column = jnp.concatenate([asked[:, g + k : g + k + 1] for k in range(group)], axis=0)
         found = dot((column == ids).astype(BF), table[...]).astype(BF)
         for k in range(group):
-            out[g + k] = found[k * capacity : (k + 1) * capacity, :]
+            found_s[g + k] = found[k * capacity : (k + 1) * capacity, :]
+        cut = pl.ds(g, group)
+        sends.append(pltpu.make_async_copy(found_s.at[cut], out.at[cut], sems.at[g // group]))
+        sends[-1].start()
+    for send in sends:
+        send.wait()
 
 
 def rank_kernel(target, returned, bias, out, *, first):
@@ -449,7 +455,8 @@
     )(item_features, after(item_proj, began))
     served = call(
         functools.partial(serve_kernel, group=4), "serve",
-        shape((owner_count, capacity, columns), BF), [VMEM] * 2, VMEM, limit=16,
+        shape((owner_count, capacity, columns), BF), [VMEM] * 2, HBM,
+        (pltpu.VMEM((owner_count, capacity, columns), BF), DMA((owner_count // 4,))), limit=58,
         flops=2 * owner_count * capacity * item_features.shape[0] * columns, moved=4_000_000,
     )(wanted, table)
     returned = lax.all_to_all(served, "dp", split_axis=0, concat_axis=0, tiled=True)

time: 128 us -> 128 us (level)
  local copies, waits for them, and re-layouts: 14.3 us -> 12.4 us
    unnamed x58 -> x54, local copies, waits for them, and re-layouts: 14.3 us -> 12.4 us
  transfers between devices with their start and end apart: 21 -> 21, of which waited for: 9 -> 7; matrix products, arithmetic and copies ran while one was open for 0% -> 0% of each run, Pallas kernels for 15% -> 15%
where the time goes in v2:
time: 128 us; the launch traced here: 127 us
  starting transfers between devices  42.1 us (33%)
  waiting for transfers between devices  37.3 us (29%)
  Pallas kernels  34.3 us (27%)
  local copies, waits for them, and re-layouts  12.4 us (10%)
    ppermute x18, waiting for transfers between devices, shift(): lax.ppermute(value, axis, [(i, (i + by) % size) for i in range(size)])  34.6 us
    ppermute x18, starting transfers between devices, shift(): lax.ppermute(value, axis, [(i, (i + by) % size) for i in range(size)])  22.5 us
    unnamed x54, local copies, waits for them, and re-layouts  12.4 us
    all_to_all x1, starting transfers between devices, body(): lax.all_to_all(outgoing, 'dp', split_axis=0, concat_axis=0, tiled=True)  11.3 us
    pallas_call x2, Pallas kernels, ranked(): call(functools.partial(rank_kernel, first=first), f'rank{first}', shape((...  6.74 us
    all_to_all x1, starting transfers between devices, body(): lax.all_to_all(served, 'dp', split_axis=0, concat_axis=0, tiled=True)  6.6 us
    pallas_call x1, Pallas kernels, body(): call(functools.partial(serve_kernel, group=4), 'serve', shape((owner_coun...  5.57 us
    pallas_call x1, Pallas kernels, body(): call(second_kernel, 'ffn1', quarter + (shape((own, width), BF),), [VMEM]...  3.8 us
  transfers between devices with their start and end apart: 21, of which 7 were waited for; matrix products, arithmetic and copies ran while one was open for 0% of the time, Pallas kernels for 15%

profile of v2, /device:TPU:1, one launch (start us, length us, event | category | flops | bytes accessed | tf_op | source)
XLA Modules:
  0.0 127.1 jit_solution(1814110332438070789)
XLA Ops:
  0.6 2.2 %copy-done.15 = bf16[2048,1024]{1,0:T(8,128)(2,1)S(1)} copy-done((bf16[2048,1024]{1,0:T(8,128)(2,1)S(1)}, bf16[2048,1024]{1,0:T(8,128)(2,1)}, u32[]{:S(2)}) %copy-start.15) | copy-done | bytes 4194328
  2.8 0.8 copy-done.18
  3.7 0.7 copy-done.21
  4.4 0.7 copy-done.22
  5.1 0.7 copy-done.23
  5.8 3.3 %start.1 = (s32[32,96]{1,0:T(8,128)S(1)}, s32[8,384]{1,0:T(8,128)S(1)}, bf16[16,2048]{1,0:T(8,128)(2,1)S(1)}, bf16[16,2048]{1,0:T(8,128)(2,1)S(1)}, f32[1,2048]{...) custom-call(s32[4,1,384]{2,1,0:T(1,128)S(1)} %bitcast.11, s32[4,384]{1,0:T(4,128)S(1)} %copy-done.23, ...), custom_call_target="tpu_custom_call" | custom-call | flops 53687091200 | bytes 1000000 | tf_op jit(solution)/shard_map/start/pallas_call | solution.py:366
  9.0 0.6 copy-done.12
  9.6 0.6 copy-done.25
  10.2 2.1 %collective-permute-start = (bf16[16,2048]{1,0:T(8,128)(2,1)S(1)}, bf16[16,2048]{1,0:T(8,128)(2,1)S(1)}, u32[]{:S(2)}, u32[]{:S(2)}) collective-permute-start(bf16[16,2048]{1,0:T(8,128)(2,1)S(1)} %get-tuple-element.41.t0), channel_id=1, source_target_pairs={{0,1},{1,2},{2,3},{3,0},{4,5},{5,6},{6,7},{7,4},{8,9},{9,10},{10,1... | collective-permute-start | bytes 196616 | tf_op jit(solution)/shard_map/ppermute | solution.py:44
  12.4 2.6 %collective-permute-start.1 = (bf16[16,2048]{1,0:T(8,128)(2,1)S(1)}, bf16[16,2048]{1,0:T(8,128)(2,1)S(1)}, u32[]{:S(2)}, u32[]{:S(2)}) collective-permute-start(bf16[16,2048]{1,0:T(8,128)(2,1)S(1)} %get-tuple-element.41.t0), channel_id=1, source_target_pairs={{0,2},{1,3},{2,0},{3,1},{4,6},{5,7},{6,4},{7,5},{8,10},{9,11},{10,... | collective-permute-start | bytes 196616 | tf_op jit(solution)/shard_map/ppermute | solution.py:44
  15.0 1.1 collective-permute-start.2
  16.1 2.1 %prepare.1 = (bf16[256,2048]{1,0:T(8,128)(2,1)S(1)}, bf16[64,2048]{1,0:T(8,128)(2,1)S(1)}, bf16[64,2048]{1,0:T(8,128)(2,1)S(1)}, f32[16,2048]{1,0:T(8,128)S(1)},...) custom-call(s32[16,4,16]{2,1,0:T(4,128)S(1)} %copy-done.19, ...), custom_call_target="tpu_custom_call" | custom-call | flops 419430400 | bytes 3000000 | tf_op jit(solution)/shard_map/prepare/pallas_call | solution.py:385
  18.2 0.6 copy-done.10
  18.9 3.8 %ffn1.1 = (bf16[64,2048]{1,0:T(8,128)(2,1)S(1)}, bf16[64,2048]{1,0:T(8,128)(2,1)}, bf16[64,2048]{1,0:T(8,128)(2,1)}, bf16[64,2048]{1,0:T(8,128)(2,1)}, bf16[64,2048]{1,0:T(8,128)(2,1)S(1)}) custom-call(bf16[16,2048]{1,0:T(8,128)(2,1)S(1)} %get-tuple-element.40.prompt, bf16[16,2048]{1,0:T(8,128)(2,1)S(1)} %get-tuple-element.41.t0, ...), custom_call_target="tpu_custom_call" | custom-call | flops 2147483648 | bytes 104857600 | tf_op jit(solution)/shard_map/ffn1/pallas_call | solution.py:412
  22.7 0.7 copy-done.4
  23.8 2.3 %collective-permute-start.4 = (bf16[64,2048]{1,0:T(8,128)(2,1)}, bf16[64,2048]{1,0:T(8,128)(2,1)}, u32[]{:S(2)}, u32[]{:S(2)}) collective-permute-start(bf16[64,2048]{1,0:T(8,128)(2,1)} %get-tuple-element.49), channel_id=1, source_target_pairs={{0,2},{1,3},{2,0},{3,1},{4,6},{5,7},{6,4},{7,5},{8,10},{9,11},{10,... | collective-permute-start | bytes 786440 | tf_op jit(solution)/shard_map/ppermute | solution.py:44
  26.2 11.3 %all-to-all-start = ((s32[32,1,96]{2,1,0:T(1,128)}), s32[32,1,96]{2,1,0:T(1,128)}, u32[]{:S(2)}, u32[]{:S(2)}) async-start(s32[32,1,96]{2,1,0:T(1,128)} %bitcast.8), calls=%async_computation | async-start | bytes 32768 | tf_op jit(solution)/shard_map/all_to_all | solution.py:420
  37.5 1.2 table.3
  38.8 0.9 copy-done.3
  39.7 0.9 copy-done.5
  40.6 0.7 copy-done.11
  41.4 1.6 %owner1.1 = (bf16[64,2048]{1,0:T(8,128)(2,1)S(1)}, bf16[64,2048]{1,0:T(8,128)(2,1)S(1)}) custom-call(bf16[64,2048]{1,0:T(8,128)(2,1)S(1)} %get-tuple-element.47.t0, bf16[64,2048]{1,0:T(8,128)(2,1)} %collective-permute-done.3.t1, bf16[64,2048]{1,0:T(8,128)(2,1)} %collective-permute-done.4.t2, bf16[64,2048]{1,0:T(8,128)(2,1)} %collective-permute-done.5.t3, ...), custom_call_target="tpu_custom_call" | custom-call | flops 16777216 | bytes 2000000 | tf_op jit(solution)/shard_map/owner1/pallas_call | solution.py:422
  42.9 2.7 %all-to-all-done = s32[32,1,96]{2,1,0:T(1,128)} async-done(((s32[32,1,96]{2,1,0:T(1,128)}), s32[32,1,96]{2,1,0:T(1,128)}, u32[]{:S(2)}, u32[]{:S(2)}) %all-to-all-start) | async-done | bytes 12320 | tf_op jit(solution)/shard_map/all_to_all | solution.py:420
  45.7 5.6 %serve.1 = bf16[32,96,384]{2,1,0:T(8,128)(2,1)} custom-call(s32[32,96]{1,0:T(8,128)} %bitcast.4.wanted, bf16[1024,384]{1,0:T(8,128)(2,1)} %copy-done.3), custom_call_target="tpu_custom_call" | custom-call | flops 2415919104 | bytes 4000000 | tf_op jit(solution)/shard_map/serve/pallas_call | solution.py:456
  51.2 6.6 %all-to-all-start.1 = ((bf16[32,96,384]{2,1,0:T(8,128)(2,1)}), bf16[32,96,384]{2,1,0:T(8,128)(2,1)S(1)}, u32[]{:S(2)}, u32[]{:S(2)}) async-start(bf16[32,96,384]{2,1,0:T(8,128)(2,1)} %serve.1), calls=%async_computation.1 | async-start | bytes 4718592 | tf_op jit(solution)/shard_map/all_to_all | solution.py:462
  57.8 3.5 %collective-permute-start.6 = (bf16[64,2048]{1,0:T(8,128)(2,1)S(1)}, bf16[64,2048]{1,0:T(8,128)(2,1)S(1)}, u32[]{:S(2)}, u32[]{:S(2)}) collective-permute-start(bf16[64,2048]{1,0:T(8,128)(2,1)S(1)} %get-tuple-element.54.refs_0_), channel_id=1, source_target_pairs={{0,3},{1,0},{2,1},{3,2},{4,7},{5,4},{6,5},{7,6},{8,11},{9,8},{10,9... | collective-permute-start | bytes 786440 | tf_op jit(solution)/shard_map/ppermute | solution.py:44
  61.3 0.7 collective-permute-start.8
  62.0 2.2 %copy-done.16 = bf16[2048,1024]{1,0:T(8,128)(2,1)S(1)} copy-done((bf16[2048,1024]{1,0:T(8,128)(2,1)S(1)}, bf16[2048,1024]{1,0:T(8,128)(2,1)}, u32[]{:S(2)}) %copy-start.16) | copy-done | bytes 4194328
  64.2 2.5 %load.1 = (bf16[2048,1024]{1,0:T(8,128)(2,1)S(1)}, bf16[1024,2048]{1,0:T(8,128)(2,1)S(1)}) custom-call(bf16[2048,1024]{1,0:T(8,128)(2,1)S(1)} %copy-done.16, bf16[1024,2048]{1,0:T(8,128)(2,1)} %down.2), custom_call_target="tpu_custom_call" | custom-call | flops 10737418240 | bytes 1000000 | tf_op jit(solution)/shard_map/load/pallas_call | solution.py:427
  66.7 5.5 %collective-permute-done.6.refs_1_ = bf16[64,2048]{1,0:T(8,128)(2,1)S(1)} collective-permute-done((bf16[64,2048]{1,0:T(8,128)(2,1)S(1)}, bf16[64,2048]{1,0:T(8,128)(2,1)S(1)}, u32[]{:S(2)}, u32[]{:S(2)}) %collective-permute-start.6) | collective-permute-done | bytes 262176 | tf_op jit(solution)/shard_map/ppermute | solution.py:44
  72.2 3.8 %collective-permute-done.8.refs_3_ = bf16[64,2048]{1,0:T(8,128)(2,1)S(1)} collective-permute-done((bf16[64,2048]{1,0:T(8,128)(2,1)S(1)}, bf16[64,2048]{1,0:T(8,128)(2,1)S(1)}, u32[]{:S(2)}, u32[]{:S(2)}) %collective-permute-start.8) | collective-permute-done | bytes 262176 | tf_op jit(solution)/shard_map/ppermute | solution.py:44
  76.0 2.5 %ffn2.1 = (bf16[64,2048]{1,0:T(8,128)(2,1)S(1)}, bf16[64,2048]{1,0:T(8,128)(2,1)S(1)}, bf16[64,2048]{1,0:T(8,128)(2,1)S(1)}, bf16[64,2048]{1,0:T(8,128)(2,1)S(1)}) custom-call(bf16[64,2048]{1,0:T(8,128)(2,1)S(1)} %get-tuple-element.54.refs_0_, bf16[64,2048]{1,0:T(8,128)(2,1)S(1)} %collective-permute-done.6.refs_1_, ...), custom_call_target="tpu_custom_call" | custom-call | flops 2147483648 | bytes 104857600 | tf_op jit(solution)/shard_map/ffn2/pallas_call | solution.py:433
  78.6 1.0 collective-permute-start.10
  79.6 1.7 %collective-permute-start.11 = (bf16[64,2048]{1,0:T(8,128)(2,1)S(1)}, bf16[64,2048]{1,0:T(8,128)(2,1)S(1)}, u32[]{:S(2)}, u32[]{:S(2)}) collective-permute-start(bf16[64,2048]{1,0:T(8,128)(2,1)S(1)} %get-tuple-element.62), channel_id=1, source_target_pairs={{0,3},{1,0},{2,1},{3,2},{4,7},{5,4},{6,5},{7,6},{8,11},{9,8},{10,9... | collective-permute-start | bytes 786440 | tf_op jit(solution)/shard_map/ppermute | solution.py:44
  81.3 11.0 %collective-permute-done.9.t1 = bf16[64,2048]{1,0:T(8,128)(2,1)S(1)} collective-permute-done((bf16[64,2048]{1,0:T(8,128)(2,1)S(1)}, bf16[64,2048]{1,0:T(8,128)(2,1)S(1)}, u32[]{:S(2)}, u32[]{:S(2)}) %collective-permute-start.9) | collective-permute-done | bytes 262176 | tf_op jit(solution)/shard_map/ppermute | solution.py:44
  92.7 0.5 owner2.1
  93.2 3.4 %collective-permute-start.12 = (bf16[64,2048]{1,0:T(8,128)(2,1)S(1)}, bf16[64,2048]{1,0:T(8,128)(2,1)S(1)}, u32[]{:S(2)}, u32[]{:S(2)}) collective-permute-start(bf16[64,2048]{1,0:T(8,128)(2,1)S(1)} %get-tuple-element.68.refs_0_), channel_id=1, source_target_pairs={{0,3},{1,0},{2,1},{3,2},{4,7},{5,4},{6,5},{7,6},{8,11},{9,8},{10,9... | collective-permute-start | bytes 786440 | tf_op jit(solution)/shard_map/ppermute | solution.py:44
  96.6 0.9 collective-permute-start.14
  97.4 9.5 %collective-permute-done.12.refs_1_ = bf16[64,2048]{1,0:T(8,128)(2,1)S(1)} collective-permute-done((bf16[64,2048]{1,0:T(8,128)(2,1)S(1)}, bf16[64,2048]{1,0:T(8,128)(2,1)S(1)}, u32[]{:S(2)}, u32[]{:S(2)}) %collective-permute-start.12) | collective-permute-done | bytes 262176 | tf_op jit(solution)/shard_map/ppermute | solution.py:44
  106.9 4.4 %collective-permute-done.14.refs_3_ = bf16[64,2048]{1,0:T(8,128)(2,1)S(1)} collective-permute-done((bf16[64,2048]{1,0:T(8,128)(2,1)S(1)}, bf16[64,2048]{1,0:T(8,128)(2,1)S(1)}, u32[]{:S(2)}, u32[]{:S(2)}) %collective-permute-start.14) | collective-permute-done | bytes 262176 | tf_op jit(solution)/shard_map/ppermute | solution.py:44
  111.3 2.1 %ffn3.1.t0 = bf16[16,2048]{1,0:T(8,128)(2,1)S(1)} custom-call(bf16[64,2048]{1,0:T(8,128)(2,1)S(1)} %get-tuple-element.68.refs_0_, bf16[64,2048]{1,0:T(8,128)(2,1)S(1)} %collective-permute-done.12.refs_1_, bf16[64,2048]{1,0:T(8,128)(2,1)S(1)} %collective-permute-done.13.refs_2_, bf16[64,2048]{1,0:T(8,128)(2,1)S(1)} %collective-permute-done.14.refs_3_, ...), custom_call_target="tpu_custom_call" | custom-call | flops 2147483648 | bytes 104857600 | tf_op jit(solution)/shard_map/ffn3/pallas_call | solution.py:446
  113.5 0.7 collective-permute-start.16
  114.2 2.0 %collective-permute-start.17 = (bf16[16,2048]{1,0:T(8,128)(2,1)S(1)}, bf16[16,2048]{1,0:T(8,128)(2,1)S(1)}, u32[]{:S(2)}, u32[]{:S(2)}) collective-permute-start(bf16[16,2048]{1,0:T(8,128)(2,1)S(1)} %ffn3.1.t0), channel_id=1, source_target_pairs={{0,3},{1,0},{2,1},{3,2},{4,7},{5,4},{6,5},{7,6},{8,11},{9,8},{10,9... | collective-permute-start | bytes 196616 | tf_op jit(solution)/shard_map/ppermute | solution.py:44
  116.2 3.4 %rank0.1.units0 = f32[2,256,128]{2,1,0:T(8,128)S(1)} custom-call(s32[8,384]{1,0:T(8,128)S(1)} %copy-done.26, bf16[32,96,384]{2,1,0:T(8,128)(2,1)S(1)} %all-to-all-done.1.returned, f32[1,256]{1,0:T(1,128)S(1)} %bitcast.12), custom_call_target="tpu_custom_call" | custom-call | flops 1811939328 | bytes 4000000 | tf_op jit(solution)/shard_map/rank0/pallas_call | solution.py:465
  119.6 0.7 pool.1
  120.3 1.7 %collective-permute-start.18 = (bf16[16,2048]{1,0:T(8,128)(2,1)}, bf16[16,2048]{1,0:T(8,128)(2,1)S(1)}, u32[]{:S(2)}, u32[]{:S(2)}) collective-permute-start(bf16[16,2048]{1,0:T(8,128)(2,1)} %pool.1), channel_id=1, source_target_pairs={{0,128},{128,0},{1,129},{129,1},{2,130},{130,2},{3,131},{131,3},{4... | collective-permute-start | bytes 196616 | tf_op jit(solution)/shard_map/ppermute | solution.py:50
  122.0 3.4 %rank2.1.units1 = f32[2,256,128]{2,1,0:T(8,128)S(1)} custom-call(s32[8,384]{1,0:T(8,128)S(1)} %copy-done.26, bf16[32,96,384]{2,1,0:T(8,128)(2,1)S(1)} %all-to-all-done.1.returned, f32[1,256]{1,0:T(1,128)S(1)} %bitcast.13), custom_call_target="tpu_custom_call" | custom-call | flops 1811939328 | bytes 4000000 | tf_op jit(solution)/shard_map/rank2/pallas_call | solution.py:465
  125.4 1.7 %logit.1 = f32[4,128]{1,0:T(4,128)} custom-call(s32[4]{0:T(128)S(1)} %copy-done.14, bf16[16,2048]{1,0:T(8,128)(2,1)S(1)} %collective-permute-done.18.users, bf16[2048,256]{1,0:T(8,128)(2,1)S(1)} %copy-done.1, f32[2,256,128]{2,1,0:T(8,128)S(1)} %rank0.1.units0, f32[2,256,128]{2,1,0:T(8,128)S(1)} %rank2.1.units1, f32[1,256]{1,0:T(1,128)S(1)} %bitcast.9), custom_call_target="tpu_custom_call" | custom-call | flops 20000000 | bytes 1600000 | tf_op jit(solution)/shard_map/logit/pallas_call | solution.py:480
  (62 shorter events, 1.1 us)
Async XLA Ops:
  0.6 2.2 %copy-start.15 = (bf16[2048,1024]{1,0:T(8,128)(2,1)S(1)}, bf16[2048,1024]{1,0:T(8,128)(2,1)}, u32[]{:S(2)}) copy-start(bf16[2048,1024]{1,0:T(8,128)(2,1)} %up.2) | copy-start | bytes 12582916
  2.8 0.8 copy-start.18
  3.7 0.7 copy-start.21
  4.4 0.7 copy-start.22
  5.1 0.7 copy-start.23
  5.7 10.3 %copy-start.17 = (bf16[256,2048]{1,0:T(8,128)(2,1)S(1)}, bf16[256,2048]{1,0:T(8,128)(2,1)}, u32[]{:S(2)}) copy-start(bf16[256,2048]{1,0:T(8,128)(2,1)} %table.2) | copy-start | bytes 3145732
  5.7 10.3 %copy-start.19 = (s32[16,4,16]{2,1,0:T(4,128)S(1)}, s32[16,4,16]{2,1,0:T(4,128)}, u32[]{:S(2)}) copy-start(s32[16,4,16]{2,1,0:T(4,128)} %code.1) | copy-start | bytes 12292
  5.7 10.3 %copy-start.20 = (s32[16,4,16]{2,1,0:T(4,128)S(1)}, s32[16,4,16]{2,1,0:T(4,128)}, u32[]{:S(2)}) copy-start(s32[16,4,16]{2,1,0:T(4,128)} %parent) | copy-start | bytes 12292
  9.0 0.6 copy-start.12
  9.6 0.6 copy-start.25
  10.2 8.6 %collective-permute-start = (bf16[16,2048]{1,0:T(8,128)(2,1)S(1)}, bf16[16,2048]{1,0:T(8,128)(2,1)S(1)}, u32[]{:S(2)}, u32[]{:S(2)}) collective-permute-start(bf16[16,2048]{1,0:T(8,128)(2,1)S(1)} %get-tuple-element.41.t0), channel_id=1, source_target_pairs={{0,1},{1,2},{2,3},{3,0},{4,5},{5,6},{6,7},{7,4},{8,9},{9,10},{10,1... | collective-permute-start | bytes 196616 | tf_op jit(solution)/shard_map/ppermute | solution.py:44
  12.4 6.5 %collective-permute-start.1 = (bf16[16,2048]{1,0:T(8,128)(2,1)S(1)}, bf16[16,2048]{1,0:T(8,128)(2,1)S(1)}, u32[]{:S(2)}, u32[]{:S(2)}) collective-permute-start(bf16[16,2048]{1,0:T(8,128)(2,1)S(1)} %get-tuple-element.41.t0), channel_id=1, source_target_pairs={{0,2},{1,3},{2,0},{3,1},{4,6},{5,7},{6,4},{7,5},{8,10},{9,11},{10,... | collective-permute-start | bytes 196616 | tf_op jit(solution)/shard_map/ppermute | solution.py:44
  15.0 3.9 %collective-permute-start.2 = (bf16[16,2048]{1,0:T(8,128)(2,1)S(1)}, bf16[16,2048]{1,0:T(8,128)(2,1)S(1)}, u32[]{:S(2)}, u32[]{:S(2)}) collective-permute-start(bf16[16,2048]{1,0:T(8,128)(2,1)S(1)} %get-tuple-element.41.t0), channel_id=1, source_target_pairs={{0,3},{1,0},{2,1},{3,2},{4,7},{5,4},{6,5},{7,6},{8,11},{9,8},{10,9... | collective-permute-start | bytes 196616 | tf_op jit(solution)/shard_map/ppermute | solution.py:44
  18.2 0.6 copy-start.10
  18.8 3.8 %copy-start.6 = (bf16[64,2048]{1,0:T(8,128)(2,1)}, bf16[64,2048]{1,0:T(8,128)(2,1)S(1)}, u32[]{:S(2)}) copy-start(bf16[64,2048]{1,0:T(8,128)(2,1)S(1)} %get-tuple-element.65.code_rows) | copy-start | bytes 786436
  18.8 3.8 %copy-start.8 = (bf16[64,64]{1,0:T(8,128)(2,1)}, bf16[64,64]{1,0:T(8,128)(2,1)S(1)}, u32[]{:S(2)}) copy-start(bf16[64,64]{1,0:T(8,128)(2,1)S(1)} %get-tuple-element.64.chosen) | copy-start | bytes 24580
  18.8 18.7 %copy-start = (bf16[1024,1024]{1,0:T(8,128)(2,1)S(1)}, bf16[1024,1024]{1,0:T(8,128)(2,1)}, u32[]{:S(2)}) copy-start(bf16[1024,1024]{1,0:T(8,128)(2,1)} %features.1) | copy-start | bytes 6291460
  18.9 18.7 %copy-start.2 = (bf16[1024,384]{1,0:T(8,128)(2,1)S(1)}, bf16[1024,384]{1,0:T(8,128)(2,1)}, u32[]{:S(2)}) copy-start(bf16[1024,384]{1,0:T(8,128)(2,1)} %proj) | copy-start | bytes 2359300
  22.7 0.7 copy-start.4
  23.4 16.3 %collective-permute-start.3 = (bf16[64,2048]{1,0:T(8,128)(2,1)}, bf16[64,2048]{1,0:T(8,128)(2,1)}, u32[]{:S(2)}, u32[]{:S(2)}) collective-permute-start(bf16[64,2048]{1,0:T(8,128)(2,1)} %get-tuple-element.48), channel_id=1, source_target_pairs={{0,1},{1,2},{2,3},{3,0},{4,5},{5,6},{6,7},{7,4},{8,9},{9,10},{10,1... | collective-permute-start | bytes 786440 | tf_op jit(solution)/shard_map/ppermute | solution.py:44
  23.8 15.9 %collective-permute-start.4 = (bf16[64,2048]{1,0:T(8,128)(2,1)}, bf16[64,2048]{1,0:T(8,128)(2,1)}, u32[]{:S(2)}, u32[]{:S(2)}) collective-permute-start(bf16[64,2048]{1,0:T(8,128)(2,1)} %get-tuple-element.49), channel_id=1, source_target_pairs={{0,2},{1,3},{2,0},{3,1},{4,6},{5,7},{6,4},{7,5},{8,10},{9,11},{10,... | collective-permute-start | bytes 786440 | tf_op jit(solution)/shard_map/ppermute | solution.py:44
  26.1 13.6 %collective-permute-start.5 = (bf16[64,2048]{1,0:T(8,128)(2,1)}, bf16[64,2048]{1,0:T(8,128)(2,1)}, u32[]{:S(2)}, u32[]{:S(2)}) collective-permute-start(bf16[64,2048]{1,0:T(8,128)(2,1)} %get-tuple-element.50), channel_id=1, source_target_pairs={{0,3},{1,0},{2,1},{3,2},{4,7},{5,4},{6,5},{7,6},{8,11},{9,8},{10,9... | collective-permute-start | bytes 786440 | tf_op jit(solution)/shard_map/ppermute | solution.py:44
  26.2 19.5 %all-to-all-start = ((s32[32,1,96]{2,1,0:T(1,128)}), s32[32,1,96]{2,1,0:T(1,128)}, u32[]{:S(2)}, u32[]{:S(2)}) async-start(s32[32,1,96]{2,1,0:T(1,128)} %bitcast.8), calls=%async_computation | async-start | bytes 32768 | tf_op jit(solution)/shard_map/all_to_all | solution.py:420
  38.8 0.9 copy-start.3
  39.7 1.0 copy-start.5
  40.6 0.7 copy-start.11
  51.2 64.9 %all-to-all-start.1 = ((bf16[32,96,384]{2,1,0:T(8,128)(2,1)}), bf16[32,96,384]{2,1,0:T(8,128)(2,1)S(1)}, u32[]{:S(2)}, u32[]{:S(2)}) async-start(bf16[32,96,384]{2,1,0:T(8,128)(2,1)} %serve.1), calls=%async_computation.1 | async-start | bytes 4718592 | tf_op jit(solution)/shard_map/all_to_all | solution.py:462
  57.8 14.3 %collective-permute-start.6 = (bf16[64,2048]{1,0:T(8,128)(2,1)S(1)}, bf16[64,2048]{1,0:T(8,128)(2,1)S(1)}, u32[]{:S(2)}, u32[]{:S(2)}) collective-permute-start(bf16[64,2048]{1,0:T(8,128)(2,1)S(1)} %get-tuple-element.54.refs_0_), channel_id=1, source_target_pairs={{0,3},{1,0},{2,1},{3,2},{4,7},{5,4},{6,5},{7,6},{8,11},{9,8},{10,9... | collective-permute-start | bytes 786440 | tf_op jit(solution)/shard_map/ppermute | solution.py:44
  61.3 10.9 %collective-permute-start.7 = (bf16[64,2048]{1,0:T(8,128)(2,1)S(1)}, bf16[64,2048]{1,0:T(8,128)(2,1)S(1)}, u32[]{:S(2)}, u32[]{:S(2)}) collective-permute-start(bf16[64,2048]{1,0:T(8,128)(2,1)S(1)} %get-tuple-element.54.refs_0_), channel_id=1, source_target_pairs={{0,2},{1,3},{2,0},{3,1},{4,6},{5,7},{6,4},{7,5},{8,10},{9,11},{10,... | collective-permute-start | bytes 786440 | tf_op jit(solution)/shard_map/ppermute | solution.py:44
  61.3 14.6 %collective-permute-start.8 = (bf16[64,2048]{1,0:T(8,128)(2,1)S(1)}, bf16[64,2048]{1,0:T(8,128)(2,1)S(1)}, u32[]{:S(2)}, u32[]{:S(2)}) collective-permute-start(bf16[64,2048]{1,0:T(8,128)(2,1)S(1)} %get-tuple-element.54.refs_0_), channel_id=1, source_target_pairs={{0,1},{1,2},{2,3},{3,0},{4,5},{5,6},{6,7},{7,4},{8,9},{9,10},{10,1... | collective-permute-start | bytes 786440 | tf_op jit(solution)/shard_map/ppermute | solution.py:44
  62.0 2.2 %copy-start.16 = (bf16[2048,1024]{1,0:T(8,128)(2,1)S(1)}, bf16[2048,1024]{1,0:T(8,128)(2,1)}, u32[]{:S(2)}) copy-start(bf16[2048,1024]{1,0:T(8,128)(2,1)} %up.2) | copy-start | bytes 12582916
  76.0 16.7 %copy-start.7 = (bf16[64,2048]{1,0:T(8,128)(2,1)S(1)}, bf16[64,2048]{1,0:T(8,128)(2,1)}, u32[]{:S(2)}) copy-start(bf16[64,2048]{1,0:T(8,128)(2,1)} %copy-done.6) | copy-start | bytes 786436
  76.0 16.7 %copy-start.9 = (bf16[64,64]{1,0:T(8,128)(2,1)S(1)}, bf16[64,64]{1,0:T(8,128)(2,1)}, u32[]{:S(2)}) copy-start(bf16[64,64]{1,0:T(8,128)(2,1)} %copy-done.8) | copy-start | bytes 24580
  78.5 13.8 %collective-permute-start.9 = (bf16[64,2048]{1,0:T(8,128)(2,1)S(1)}, bf16[64,2048]{1,0:T(8,128)(2,1)S(1)}, u32[]{:S(2)}, u32[]{:S(2)}) collective-permute-start(bf16[64,2048]{1,0:T(8,128)(2,1)S(1)} %get-tuple-element.60), channel_id=1, source_target_pairs={{0,1},{1,2},{2,3},{3,0},{4,5},{5,6},{6,7},{7,4},{8,9},{9,10},{10,1... | collective-permute-start | bytes 786440 | tf_op jit(solution)/shard_map/ppermute | solution.py:44
  78.6 13.7 %collective-permute-start.10 = (bf16[64,2048]{1,0:T(8,128)(2,1)S(1)}, bf16[64,2048]{1,0:T(8,128)(2,1)S(1)}, u32[]{:S(2)}, u32[]{:S(2)}) collective-permute-start(bf16[64,2048]{1,0:T(8,128)(2,1)S(1)} %get-tuple-element.61), channel_id=1, source_target_pairs={{0,2},{1,3},{2,0},{3,1},{4,6},{5,7},{6,4},{7,5},{8,10},{9,11},{10,... | collective-permute-start | bytes 786440 | tf_op jit(solution)/shard_map/ppermute | solution.py:44
  79.6 13.1 %collective-permute-start.11 = (bf16[64,2048]{1,0:T(8,128)(2,1)S(1)}, bf16[64,2048]{1,0:T(8,128)(2,1)S(1)}, u32[]{:S(2)}, u32[]{:S(2)}) collective-permute-start(bf16[64,2048]{1,0:T(8,128)(2,1)S(1)} %get-tuple-element.62), channel_id=1, source_target_pairs={{0,3},{1,0},{2,1},{3,2},{4,7},{5,4},{6,5},{7,6},{8,11},{9,8},{10,9... | collective-permute-start | bytes 786440 | tf_op jit(solution)/shard_map/ppermute | solution.py:44
  93.2 13.7 %collective-permute-start.12 = (bf16[64,2048]{1,0:T(8,128)(2,1)S(1)}, bf16[64,2048]{1,0:T(8,128)(2,1)S(1)}, u32[]{:S(2)}, u32[]{:S(2)}) collective-permute-start(bf16[64,2048]{1,0:T(8,128)(2,1)S(1)} %get-tuple-element.68.refs_0_), channel_id=1, source_target_pairs={{0,3},{1,0},{2,1},{3,2},{4,7},{5,4},{6,5},{7,6},{8,11},{9,8},{10,9... | collective-permute-start | bytes 786440 | tf_op jit(solution)/shard_map/ppermute | solution.py:44
  96.5 10.4 %collective-permute-start.13 = (bf16[64,2048]{1,0:T(8,128)(2,1)S(1)}, bf16[64,2048]{1,0:T(8,128)(2,1)S(1)}, u32[]{:S(2)}, u32[]{:S(2)}) collective-permute-start(bf16[64,2048]{1,0:T(8,128)(2,1)S(1)} %get-tuple-element.68.refs_0_), channel_id=1, source_target_pairs={{0,2},{1,3},{2,0},{3,1},{4,6},{5,7},{6,4},{7,5},{8,10},{9,11},{10,... | collective-permute-start | bytes 786440 | tf_op jit(solution)/shard_map/ppermute | solution.py:44
  96.6 14.7 %collective-permute-start.14 = (bf16[64,2048]{1,0:T(8,128)(2,1)S(1)}, bf16[64,2048]{1,0:T(8,128)(2,1)S(1)}, u32[]{:S(2)}, u32[]{:S(2)}) collective-permute-start(bf16[64,2048]{1,0:T(8,128)(2,1)S(1)} %get-tuple-element.68.refs_0_), channel_id=1, source_target_pairs={{0,1},{1,2},{2,3},{3,0},{4,5},{5,6},{6,7},{7,4},{8,9},{9,10},{10,1... | collective-permute-start | bytes 786440 | tf_op jit(solution)/shard_map/ppermute | solution.py:44
  111.3 4.8 %copy-start.24 = (f32[256]{0:T(256)S(1)}, f32[256]{0:T(256)}, u32[]{:S(2)}) copy-start(f32[256]{0:T(256)} %param.28) | copy-start | bytes 3076
  111.3 4.8 %copy-start.26 = (s32[8,384]{1,0:T(8,128)S(1)}, s32[8,384]{1,0:T(8,128)}, u32[]{:S(2)}) copy-start(s32[8,384]{1,0:T(8,128)} %copy-done.25) | copy-start | bytes 36868
  113.5 6.1 %collective-permute-start.15 = (bf16[16,2048]{1,0:T(8,128)(2,1)S(1)}, bf16[16,2048]{1,0:T(8,128)(2,1)S(1)}, u32[]{:S(2)}, u32[]{:S(2)}) collective-permute-start(bf16[16,2048]{1,0:T(8,128)(2,1)S(1)} %ffn3.1.t0), channel_id=1, source_target_pairs={{0,1},{1,2},{2,3},{3,0},{4,5},{5,6},{6,7},{7,4},{8,9},{9,10},{10,1... | collective-permute-start | bytes 196616 | tf_op jit(solution)/shard_map/ppermute | solution.py:44
  113.5 6.1 %collective-permute-start.16 = (bf16[16,2048]{1,0:T(8,128)(2,1)S(1)}, bf16[16,2048]{1,0:T(8,128)(2,1)S(1)}, u32[]{:S(2)}, u32[]{:S(2)}) collective-permute-start(bf16[16,2048]{1,0:T(8,128)(2,1)S(1)} %ffn3.1.t0), channel_id=1, source_target_pairs={{0,2},{1,3},{2,0},{3,1},{4,6},{5,7},{6,4},{7,5},{8,10},{9,11},{10,... | collective-permute-start | bytes 196616 | tf_op jit(solution)/shard_map/ppermute | solution.py:44
  114.2 5.4 %collective-permute-start.17 = (bf16[16,2048]{1,0:T(8,128)(2,1)S(1)}, bf16[16,2048]{1,0:T(8,128)(2,1)S(1)}, u32[]{:S(2)}, u32[]{:S(2)}) collective-permute-start(bf16[16,2048]{1,0:T(8,128)(2,1)S(1)} %ffn3.1.t0), channel_id=1, source_target_pairs={{0,3},{1,0},{2,1},{3,2},{4,7},{5,4},{6,5},{7,6},{8,11},{9,8},{10,9... | collective-permute-start | bytes 196616 | tf_op jit(solution)/shard_map/ppermute | solution.py:44
  119.5 5.8 %copy-start.1 = (bf16[2048,256]{1,0:T(8,128)(2,1)S(1)}, bf16[2048,256]{1,0:T(8,128)(2,1)}, u32[]{:S(2)}) copy-start(bf16[2048,256]{1,0:T(8,128)(2,1)} %user_proj.1) | copy-start | bytes 3145732
  119.5 5.8 %copy-start.13 = (f32[256]{0:T(256)S(1)}, f32[256]{0:T(256)}, u32[]{:S(2)}) copy-start(f32[256]{0:T(256)} %param.29) | copy-start | bytes 3076
  119.6 5.8 %copy-start.14 = (s32[4]{0:T(128)S(1)}, s32[4]{0:T(128)}, u32[]{:S(2)}) copy-start(s32[4]{0:T(128)} %counts.1) | copy-start | bytes 52
  120.3 5.1 %collective-permute-start.18 = (bf16[16,2048]{1,0:T(8,128)(2,1)}, bf16[16,2048]{1,0:T(8,128)(2,1)S(1)}, u32[]{:S(2)}, u32[]{:S(2)}) collective-permute-start(bf16[16,2048]{1,0:T(8,128)(2,1)} %pool.1), channel_id=1, source_target_pairs={{0,128},{128,0},{1,129},{129,1},{2,130},{130,2},{3,131},{131,3},{4... | collective-permute-start | bytes 196616 | tf_op jit(solution)/shard_map/ppermute | solution.py:50
